TPU v7x, 32 devices: a whole 2x2x4 slice. The times are simulated.
32 devices in a mesh: shard: 8 (over z, x), rep: 4 (over y, core).
Axes of the slice: x: 2, y: 2, z: 4, core: 2. Of those that a mesh axis runs over, the one named last changes fastest.
Arguments:
- tokens: bfloat16 [8, 1024, 1024], P('rep', 'shard'), may hold values from -6 to 6
- lengths: int32 [8], P('rep'), may hold values from 512 to 1024, as said below
- expert_ids: int32 [8, 1024, 2], P('rep', 'shard'), may hold values from 0 to 3, all different within a row
- buckets: int32 [2047], replicated, may hold values from 0 to 31
- norm1_gain: bfloat16 [1024], P('shard'), may hold values from 0.5 to 1.5
- w_query: bfloat16 [1024, 1024], P('shard'), may hold values from -0.1875 to 0.1875
- w_key: bfloat16 [1024, 1024], P('shard'), may hold values from -0.1875 to 0.1875
- w_value: bfloat16 [1024, 1024], P('shard'), may hold values from -0.1875 to 0.1875
- w_out: bfloat16 [1024, 1024], P('shard'), may hold values from -0.75 to 0.75
- rel_bias: bfloat16 [32, 16], P(None, 'shard'), may hold values from -4 to 4
- norm2_gain: bfloat16 [1024], P('shard'), may hold values from 0.5 to 1.5
- w_router: bfloat16 [1024, 4], P('shard'), may hold values from -0.125 to 0.125
- w_gate: bfloat16 [4, 2816, 1024], P(None, 'shard'), may hold values from -0.1875 to 0.1875
- w_up: bfloat16 [4, 2816, 1024], P(None, 'shard'), may hold values from -0.1875 to 0.1875
- w_down: bfloat16 [4, 2816, 1024], P(None, 'shard'), may hold values from -0.109375 to 0.109375
- cotangent: bfloat16 [8, 1024, 1024], P('rep', 'shard'), may hold values from -6 to 6
Outputs:
- block_out: bfloat16 [8, 1024, 1024], P('rep', 'shard')
- grad_tokens: float32 [8, 1024, 1024], P('rep', 'shard')
- grad_norm1_gain: float32 [1024], P('shard')
- grad_w_query: float32 [1024, 1024], P('shard')
- grad_w_key: float32 [1024, 1024], P('shard')
- grad_w_value: float32 [1024, 1024], P('shard')
- grad_w_out: float32 [1024, 1024], P('shard')
- grad_rel_bias: float32 [32, 16], P(None, 'shard')
- grad_norm2_gain: float32 [1024], P('shard')
- grad_w_router: float32 [1024, 4], P('shard')
- grad_w_gate: float32 [4, 2816, 1024], P(None, 'shard')
- grad_w_up: float32 [4, 2816, 1024], P(None, 'shard')
- grad_w_down: float32 [4, 2816, 1024], P(None, 'shard')
Inputs may be any that keep to these rules, and one draw needn't show every extreme that they name: `lengths`: in every group of 2 consecutive sequences at least one has length 1024. `expert_ids`: the two experts of a position differ.
All inputs are finite; a program needn't handle non-finite values.
Results may differ from a plain program's by a relative error of at most 0.022.
Values may be sent and summed in bfloat16 or wider, within the bound.
No kernel may reach another device: no remote copies, remote signals or barrier semaphores. Data moves between devices by JAX's collectives and lax.ppermute only.
A program may use at most 320 MiB of HBM per device.

v0:
```python
import jax
import jax.numpy as jnp
from jax import lax
from jax.sharding import PartitionSpec as P

epsilon = 1e-06
highest = lax.Precision.HIGHEST


def rms_forward(values, gain_vec):
    factor = lax.rsqrt(jnp.mean(values * values, axis=-1, keepdims=True) + epsilon)
    return (values * factor * gain_vec, factor)


def rms_backward(values, factor, gain_vec, upstream):
    weighted = upstream * gain_vec
    grad_gain = jnp.sum(upstream * values * factor, axis=0)
    grad_values = factor * weighted - values * (factor * factor * factor) * jnp.mean(
        weighted * values, axis=-1, keepdims=True
    )
    return (grad_values, grad_gain)


def assign_slots(pair_ids, alive_pairs, expert_count, capacity):
    expert_range = jnp.arange(expert_count, dtype=jnp.int32)
    hit_table = (pair_ids[:, None] == expert_range[None, :]).astype(jnp.int32) * alive_pairs[
        :, None
    ]
    earlier = jnp.cumsum(hit_table, axis=0, dtype=jnp.int32) - hit_table
    placing = jnp.sum(earlier * hit_table, axis=1, dtype=jnp.int32)
    kept_mask = jnp.logical_and(alive_pairs > 0, placing < capacity)
    slot_index = jnp.where(kept_mask, pair_ids * capacity + placing, expert_count * capacity)
    return (slot_index, kept_mask)


def gated_unit(gate_in, up_in):
    return jax.nn.gelu(gate_in, approximate=True) * up_in


def toeplitz_rows(window, row_count, col_count):
    lead = window.shape[:-1]
    padded = jnp.concatenate([window, jnp.zeros(lead + (1,), window.dtype)], axis=-1)
    rolled = jnp.concatenate([padded[..., row_count - 1 :], padded[..., : row_count - 1]], axis=-1)
    period = row_count + col_count
    tiled = jnp.tile(rolled, (1,) * len(lead) + (row_count,))
    shaped = tiled[..., : row_count * (period - 1)].reshape(lead + (row_count, period - 1))
    return shaped[..., :col_count]


def diagonal_sums(table, row_count, col_count):
    lead = table.shape[:-2]
    period = row_count + col_count
    widened = jnp.concatenate(
        [table, jnp.zeros(lead + (row_count, row_count - 1), table.dtype)], axis=-1
    )
    flat = widened.reshape(lead + (row_count * (period - 1),))
    flat = jnp.concatenate(
        [
            jnp.zeros(lead + (row_count - 1,), table.dtype),
            flat,
            jnp.zeros(lead + (1,), table.dtype),
        ],
        axis=-1,
    )
    shaped = flat.reshape(lead + (row_count, period))
    return jnp.sum(shaped[..., : period - 1], axis=-2)


def body(
    tokens,
    lengths,
    expert_ids,
    buckets,
    norm1_gain,
    w_query,
    w_key,
    w_value,
    w_out,
    rel_bias,
    norm2_gain,
    w_router,
    w_gate,
    w_up,
    w_down,
    cotangent,
):
    seq_count, span_len, width = tokens.shape
    shards = lax.axis_size("shard")
    seq_len = span_len * shards
    my_shard = lax.axis_index("shard")
    row_count = seq_count * span_len
    expert_count = w_gate.shape[0]
    capacity = 10 * row_count // (4 * expert_count)
    slot_total = expert_count * capacity
    (
        gain_one,
        query_w,
        key_projection_weight,
        value_projection_weight,
        out_w,
        bias_table,
        gain_two,
        router_w,
    ) = (
        lax.all_gather(norm1_gain, "shard", axis=0, tiled=True),
        lax.all_gather(w_query, "shard", axis=0, tiled=True),
        lax.all_gather(w_key, "shard", axis=0, tiled=True),
        lax.all_gather(w_value, "shard", axis=0, tiled=True),
        lax.all_gather(w_out, "shard", axis=0, tiled=True),
        lax.all_gather(rel_bias, "shard", axis=1, tiled=True),
        lax.all_gather(norm2_gain, "shard", axis=0, tiled=True),
        lax.all_gather(w_router, "shard", axis=0, tiled=True),
    )
    head_count = bias_table.shape[1]
    head_size = width // head_count
    inv_root = head_size ** (-0.5)
    bucket_count = bias_table.shape[0]
    gain_one = gain_one.astype(jnp.float32)
    gain_two = gain_two.astype(jnp.float32)
    positions = my_shard * span_len + jnp.arange(span_len, dtype=jnp.int32)
    live_mask = positions[None, :] < lengths[:, None]
    live_flat = live_mask.reshape(row_count).astype(jnp.float32)
    flat_tokens = tokens.reshape(row_count, width).astype(jnp.float32)
    normed, factor_one = rms_forward(flat_tokens, gain_one)
    normed_low = normed.astype(jnp.bfloat16)
    queries = jnp.dot(normed_low, query_w, preferred_element_type=jnp.float32).astype(jnp.bfloat16)
    keys_own = jnp.dot(
        normed_low, key_projection_weight, preferred_element_type=jnp.float32
    ).astype(jnp.bfloat16)
    values_own = jnp.dot(
        normed_low, value_projection_weight, preferred_element_type=jnp.float32
    ).astype(jnp.bfloat16)
    key_all, value_all = (
        lax.all_gather(keys_own.reshape(seq_count, span_len, width), "shard", axis=1, tiled=True),
        lax.all_gather(values_own.reshape(seq_count, span_len, width), "shard", axis=1, tiled=True),
    )
    query_heads = queries.reshape(seq_count, span_len, head_count, head_size)
    key_heads = key_all.reshape(seq_count, seq_len, head_count, head_size)
    value_heads = value_all.reshape(seq_count, seq_len, head_count, head_size)
    bucket_range = jnp.arange(bucket_count, dtype=jnp.int32)
    bucket_hot = (buckets[:, None] == bucket_range[None, :]).astype(jnp.float32)
    bias_vec = jnp.einsum(
        "rb,bh->hr", bucket_hot, bias_table.astype(jnp.float32), precision=highest
    )
    key_block = min(512, seq_len)
    window_len = span_len + key_block - 1
    block_ids = jnp.arange(seq_len // key_block, dtype=jnp.int32)

    def block_scores(block_index):
        first_key = block_index * key_block
        key_rows = lax.dynamic_slice_in_dim(key_heads, first_key, key_block, 1)
        value_rows = lax.dynamic_slice_in_dim(value_heads, first_key, key_block, 1)
        product = (
            jnp.einsum("sqhd,skhd->shqk", query_heads, key_rows, preferred_element_type=jnp.float32)
            * inv_root
        )
        window_start = first_key - my_shard * span_len + seq_len - span_len
        bias_window = lax.dynamic_slice_in_dim(bias_vec, window_start, window_len, 1)
        scores = product + toeplitz_rows(bias_window, span_len, key_block)[None]
        key_pos = first_key + jnp.arange(key_block, dtype=jnp.int32)
        key_live = key_pos[None, :] < lengths[:, None]
        scores = jnp.where(key_live[:, None, None, :], scores, -1e30)
        return (scores, key_rows, value_rows, window_start)

    def max_step(running, block_index):
        top_so_far, total_so_far = running
        scores = block_scores(block_index)[0]
        new_top = jnp.maximum(top_so_far, jnp.max(scores, axis=-1))
        total_so_far = total_so_far * jnp.exp(top_so_far - new_top) + jnp.sum(
            jnp.exp(scores - new_top[..., None]), axis=-1
        )
        return ((new_top, total_so_far), None)

    start_top = jnp.full((seq_count, head_count, span_len), -1e30, jnp.float32)
    (row_top, row_total), ignored = lax.scan(
        max_step, (start_top, jnp.zeros_like(start_top)), block_ids
    )
    log_sum = row_top + jnp.log(row_total)

    def value_step(running, block_index):
        scores, key_rows, value_rows, window_start = block_scores(block_index)
        weights = jnp.exp(scores - log_sum[..., None]).astype(jnp.bfloat16)
        return (
            running
            + jnp.einsum(
                "shqk,skhd->sqhd", weights, value_rows, preferred_element_type=jnp.float32
            ),
            None,
        )

    heads_sum, ignored = lax.scan(
        value_step, jnp.zeros((seq_count, span_len, head_count, head_size), jnp.float32), block_ids
    )
    context = heads_sum.reshape(row_count, width).astype(jnp.bfloat16)
    hidden_one = flat_tokens + jnp.dot(context, out_w, preferred_element_type=jnp.float32)
    mixed_norm, factor_two = rms_forward(hidden_one, gain_two)
    mixed_low = mixed_norm.astype(jnp.bfloat16)
    logits = jnp.dot(mixed_low, router_w, preferred_element_type=jnp.float32)
    router = jax.nn.softmax(logits, axis=-1)
    pair_ids = expert_ids.reshape(row_count, 2)
    choose = (
        pair_ids[:, :, None] == jnp.arange(expert_count, dtype=jnp.int32)[None, None, :]
    ).astype(jnp.float32)
    chosen = jnp.sum(choose * router[:, None, :], axis=-1)
    pair_total = jnp.sum(chosen, axis=-1, keepdims=True)
    gate_share = chosen / pair_total
    slot_index, kept_mask = assign_slots(
        pair_ids.reshape(-1),
        jnp.repeat(live_mask.reshape(row_count).astype(jnp.int32), 2),
        expert_count,
        capacity,
    )
    kept_float = kept_mask.reshape(row_count, 2).astype(jnp.float32)
    owners = (
        jnp.zeros(slot_total + 1, jnp.int32)
        .at[slot_index]
        .set(jnp.repeat(jnp.arange(row_count, dtype=jnp.int32), 2))
    )
    filled = (
        jnp.zeros(slot_total + 1, jnp.float32).at[slot_index].set(kept_mask.astype(jnp.float32))
    )
    pair_scale = gate_share * kept_float
    slot_scale = jnp.zeros(slot_total + 1, jnp.float32).at[slot_index].set(pair_scale.reshape(-1))
    dispatched = (
        jnp.take(mixed_low, owners[:slot_total], axis=0)
        * filled[:slot_total, None].astype(jnp.bfloat16)
    ).reshape(expert_count, capacity, width)
    gate_piece = lax.all_gather(w_gate, "shard", axis=1, tiled=True)
    up_piece = lax.all_gather(w_up, "shard", axis=1, tiled=True)
    down_piece = lax.all_gather(w_down, "shard", axis=1, tiled=True)
    gate_part = jnp.einsum(
        "ecd,efd->ecf", dispatched, gate_piece, preferred_element_type=jnp.float32
    )
    up_part = jnp.einsum("ecd,efd->ecf", dispatched, up_piece, preferred_element_type=jnp.float32)
    hidden_part = gated_unit(gate_part, up_part).astype(jnp.bfloat16)
    out_sum = jnp.einsum(
        "ecf,efd->ecd", hidden_part, down_piece, preferred_element_type=jnp.float32
    )
    gate_keep = gate_part
    up_keep = up_part
    out_table = jnp.concatenate(
        [out_sum.reshape(slot_total, width), jnp.zeros((1, width), jnp.float32)], axis=0
    )
    picked = jnp.take(out_table, slot_index, axis=0).reshape(row_count, 2, width)
    expert_mix = jnp.sum(picked * pair_scale[:, :, None], axis=1)
    result = live_flat[:, None] * (hidden_one + expert_mix)
    block_out = result.astype(jnp.bfloat16).reshape(seq_count, span_len, width)
    grad_result = live_flat[:, None] * cotangent.reshape(row_count, width).astype(jnp.float32)
    grad_pairs = kept_float * jnp.sum(picked * grad_result[:, None, :], axis=-1)
    grad_chosen = (
        grad_pairs - jnp.sum(grad_pairs * gate_share, axis=1, keepdims=True)
    ) / pair_total
    grad_router = jnp.sum(grad_chosen[:, :, None] * choose, axis=1)
    grad_logits = router * (grad_router - jnp.sum(router * grad_router, axis=1, keepdims=True))
    logits_low = grad_logits.astype(jnp.bfloat16)
    router_part = jnp.einsum("nd,ne->de", mixed_low, logits_low, preferred_element_type=jnp.float32)
    grad_slots = (
        (jnp.take(grad_result, owners[:slot_total], axis=0) * slot_scale[:slot_total, None])
        .astype(jnp.bfloat16)
        .reshape(expert_count, capacity, width)
    )
    gate_piece = lax.all_gather(w_gate, "shard", axis=1, tiled=True)
    up_piece = lax.all_gather(w_up, "shard", axis=1, tiled=True)
    down_piece = lax.all_gather(w_down, "shard", axis=1, tiled=True)
    gate_part = gate_keep
    up_part = up_keep
    hidden_part, pull_unit = jax.vjp(gated_unit, gate_part, up_part)
    hidden_low = hidden_part.astype(jnp.bfloat16)
    grad_hidden = jnp.einsum(
        "ecd,efd->ecf", grad_slots, down_piece, preferred_element_type=jnp.float32
    )
    grad_gate, grad_up = pull_unit(grad_hidden)
    grad_gate = grad_gate.astype(jnp.bfloat16)
    grad_up = grad_up.astype(jnp.bfloat16)
    in_sum = jnp.einsum(
        "ecf,efd->ecd", grad_gate, gate_piece, preferred_element_type=jnp.float32
    ) + jnp.einsum("ecf,efd->ecd", grad_up, up_piece, preferred_element_type=jnp.float32)
    full_gate = jnp.einsum(
        "ecf,ecd->efd", grad_gate, dispatched, preferred_element_type=jnp.float32
    )
    full_up = jnp.einsum("ecf,ecd->efd", grad_up, dispatched, preferred_element_type=jnp.float32)
    full_down = jnp.einsum(
        "ecf,ecd->efd", hidden_low, grad_slots, preferred_element_type=jnp.float32
    )
    grad_dispatched, full_gate, full_up, full_down = (in_sum, full_gate, full_up, full_down)
    shard_gate, shard_up, shard_down = (
        lax.psum_scatter(
            full_gate.astype(jnp.bfloat16), "shard", scatter_dimension=1, tiled=True
        ).astype(jnp.float32),
        lax.psum_scatter(
            full_up.astype(jnp.bfloat16), "shard", scatter_dimension=1, tiled=True
        ).astype(jnp.float32),
        lax.psum_scatter(
            full_down.astype(jnp.bfloat16), "shard", scatter_dimension=1, tiled=True
        ).astype(jnp.float32),
    )
    in_table = jnp.concatenate(
        [grad_dispatched.reshape(slot_total, width), jnp.zeros((1, width), jnp.float32)], axis=0
    )
    grad_mixed = jnp.sum(
        jnp.take(in_table, slot_index, axis=0).reshape(row_count, 2, width), axis=1
    )
    grad_mixed = grad_mixed + jnp.einsum(
        "ne,de->nd", logits_low, router_w, preferred_element_type=jnp.float32
    )
    grad_hidden_two, gain_two_part = rms_backward(hidden_one, factor_two, gain_two, grad_mixed)
    hidden_first_gradient = grad_result + grad_hidden_two
    attn_low = hidden_first_gradient.astype(jnp.bfloat16)
    out_part = jnp.einsum("nd,ne->de", context, attn_low, preferred_element_type=jnp.float32)
    grad_heads = jnp.einsum(
        "ne,de->nd", attn_low, out_w, preferred_element_type=jnp.float32
    ).astype(jnp.bfloat16)
    grad_heads = grad_heads.reshape(seq_count, span_len, head_count, head_size)

    def delta_step(running, block_index):
        scores, key_rows, value_rows, window_start = block_scores(block_index)
        prob_table = jnp.exp(scores - log_sum[..., None])
        grad_probs = jnp.einsum(
            "sqhd,skhd->shqk", grad_heads, value_rows, preferred_element_type=jnp.float32
        )
        return (running + jnp.sum(prob_table * grad_probs, axis=-1), None)

    row_delta, ignored = lax.scan(
        delta_step, jnp.zeros((seq_count, head_count, span_len), jnp.float32), block_ids
    )

    def grad_step(running, block_index):
        grad_query, bias_sum = running
        scores, key_rows, value_rows, window_start = block_scores(block_index)
        prob_table = jnp.exp(scores - log_sum[..., None])
        grad_probs = jnp.einsum(
            "sqhd,skhd->shqk", grad_heads, value_rows, preferred_element_type=jnp.float32
        )
        grad_scores = prob_table * (grad_probs - row_delta[..., None])
        offset_sums = diagonal_sums(jnp.sum(grad_scores, axis=0), span_len, key_block)
        bucket_window = lax.dynamic_slice_in_dim(buckets, window_start, window_len, 0)
        window_hot = (bucket_window[:, None] == bucket_range[None, :]).astype(jnp.float32)
        bias_sum = bias_sum + jnp.einsum("hr,rb->bh", offset_sums, window_hot, precision=highest)
        scores_low = grad_scores.astype(jnp.bfloat16)
        grad_query = (
            grad_query
            + jnp.einsum(
                "shqk,skhd->sqhd", scores_low, key_rows, preferred_element_type=jnp.float32
            )
            * inv_root
        )
        key_piece = (
            jnp.einsum(
                "shqk,sqhd->kshd", scores_low, query_heads, preferred_element_type=jnp.float32
            )
            * inv_root
        )
        value_piece = jnp.einsum(
            "shqk,sqhd->kshd",
            prob_table.astype(jnp.bfloat16),
            grad_heads,
            preferred_element_type=jnp.float32,
        )
        return (
            (grad_query, bias_sum),
            (
                key_piece.reshape(key_block, seq_count, width),
                value_piece.reshape(key_block, seq_count, width),
            ),
        )

    grad_start = (
        jnp.zeros((seq_count, span_len, head_count, head_size), jnp.float32),
        jnp.zeros((bucket_count, head_count), jnp.float32),
    )
    (grad_query, bias_sum), (key_parts, value_parts) = lax.scan(grad_step, grad_start, block_ids)
    key_grads, value_grads = (
        lax.psum_scatter(
            key_parts.reshape(seq_len, seq_count, width).astype(jnp.bfloat16),
            "shard",
            scatter_dimension=0,
            tiled=True,
        ).astype(jnp.float32),
        lax.psum_scatter(
            value_parts.reshape(seq_len, seq_count, width).astype(jnp.bfloat16),
            "shard",
            scatter_dimension=0,
            tiled=True,
        ).astype(jnp.float32),
    )
    key_reduced_precision = key_grads.astype(jnp.bfloat16)
    value_reduced_precision = value_grads.astype(jnp.bfloat16)
    query_low = grad_query.reshape(row_count, width).astype(jnp.bfloat16)
    normalized_tensor = normed_low.reshape(seq_count, span_len, width)
    query_part = jnp.einsum("nd,ne->de", normed_low, query_low, preferred_element_type=jnp.float32)
    key_portion = jnp.einsum(
        "pva,vpw->aw", normalized_tensor, key_reduced_precision, preferred_element_type=jnp.float32
    )
    value_part = jnp.einsum(
        "pva,vpw->aw",
        normalized_tensor,
        value_reduced_precision,
        preferred_element_type=jnp.float32,
    )
    grad_normed = jnp.einsum("ne,de->nd", query_low, query_w, preferred_element_type=jnp.float32)
    grad_normed = grad_normed + jnp.einsum(
        "xrp,wp->rxw",
        key_reduced_precision,
        key_projection_weight,
        preferred_element_type=jnp.float32,
    ).reshape(row_count, width)
    grad_normed = grad_normed + jnp.einsum(
        "xrp,wp->rxw",
        value_reduced_precision,
        value_projection_weight,
        preferred_element_type=jnp.float32,
    ).reshape(row_count, width)
    grad_tokens_extra, gain_one_part = rms_backward(flat_tokens, factor_one, gain_one, grad_normed)
    grad_tokens = (hidden_first_gradient + grad_tokens_extra).reshape(seq_count, span_len, width)
    (
        share_gain_one,
        share_query,
        share_key,
        share_value,
        share_out,
        share_bias,
        share_gain_two,
        share_router,
    ) = (
        lax.psum_scatter(
            gain_one_part.astype(jnp.bfloat16), "shard", scatter_dimension=0, tiled=True
        ).astype(jnp.float32),
        lax.psum_scatter(
            query_part.astype(jnp.bfloat16), "shard", scatter_dimension=0, tiled=True
        ).astype(jnp.float32),
        lax.psum_scatter(
            key_portion.astype(jnp.bfloat16), "shard", scatter_dimension=0, tiled=True
        ).astype(jnp.float32),
        lax.psum_scatter(
            value_part.astype(jnp.bfloat16), "shard", scatter_dimension=0, tiled=True
        ).astype(jnp.float32),
        lax.psum_scatter(
            out_part.astype(jnp.bfloat16), "shard", scatter_dimension=0, tiled=True
        ).astype(jnp.float32),
        lax.psum_scatter(
            bias_sum.astype(jnp.bfloat16), "shard", scatter_dimension=1, tiled=True
        ).astype(jnp.float32),
        lax.psum_scatter(
            gain_two_part.astype(jnp.bfloat16), "shard", scatter_dimension=0, tiled=True
        ).astype(jnp.float32),
        lax.psum_scatter(
            router_part.astype(jnp.bfloat16), "shard", scatter_dimension=0, tiled=True
        ).astype(jnp.float32),
    )
    (
        total_gain_one,
        total_query,
        total_key,
        total_value,
        total_out,
        total_bias,
        total_gain_two,
        total_router,
        total_gate,
        total_up,
        total_down,
    ) = (
        lax.psum(share_gain_one.astype(jnp.bfloat16), "rep").astype(jnp.float32),
        lax.psum(share_query.astype(jnp.bfloat16), "rep").astype(jnp.float32),
        lax.psum(share_key.astype(jnp.bfloat16), "rep").astype(jnp.float32),
        lax.psum(share_value.astype(jnp.bfloat16), "rep").astype(jnp.float32),
        lax.psum(share_out.astype(jnp.bfloat16), "rep").astype(jnp.float32),
        lax.psum(share_bias.astype(jnp.bfloat16), "rep").astype(jnp.float32),
        lax.psum(share_gain_two.astype(jnp.bfloat16), "rep").astype(jnp.float32),
        lax.psum(share_router.astype(jnp.bfloat16), "rep").astype(jnp.float32),
        lax.psum(shard_gate.astype(jnp.bfloat16), "rep").astype(jnp.float32),
        lax.psum(shard_up.astype(jnp.bfloat16), "rep").astype(jnp.float32),
        lax.psum(shard_down.astype(jnp.bfloat16), "rep").astype(jnp.float32),
    )
    return (
        block_out,
        grad_tokens,
        total_gain_one,
        total_query,
        total_key,
        total_value,
        total_out,
        total_bias,
        total_gain_two,
        total_router,
        total_gate,
        total_up,
        total_down,
    )


def solution(mesh):
    placed = (
        P("rep", "shard", None),
        P("rep"),
        P("rep", "shard", None),
        P(),
        P("shard"),
        P("shard", None),
        P("shard", None),
        P("shard", None),
        P("shard", None),
        P(None, "shard"),
        P("shard"),
        P("shard", None),
        P(None, "shard", None),
        P(None, "shard", None),
        P(None, "shard", None),
        P("rep", "shard", None),
    )
    return jax.shard_map(
        body,
        mesh=mesh,
        in_specs=placed,
        out_specs=(
            P("rep", "shard", None),
            P("rep", "shard", None),
            P("shard"),
            P("shard", None),
            P("shard", None),
            P("shard", None),
            P("shard", None),
            P(None, "shard"),
            P("shard"),
            P("shard", None),
            P(None, "shard", None),
            P(None, "shard", None),
            P(None, "shard", None),
        ),
        check_vma=False,
    )
```

profile of v0, /device:TPU:1, one launch (start us, length us, event | category | flops | bytes accessed | tf_op | source)
XLA Modules:
  0.0 3931.5 jit_solution(6110642589549525552)
XLA Ops:
  9.4 18.0 all-gather
  31.0 29.4 all-gather.13.cloned.1.call-done
  63.6 46.8 %all-gather.17.cloned.1.call-done = bf16[1024,1024]{1,0:T(8,128)(2,1)} async-done(((bf16[128,1024]{1,0:T(8,128)(2,1)}), bf16[1024,1024]{1,0:T(8,128)(2,1)}) %all-gather.17.cloned.1.call-update) | async-done | bytes 2097168 | tf_op jit(solution)/shard_map/all_gather | solution.py:107
  116.9 15.2 all-gather.2
  163.2 15.5 all_gather.54
  184.4 50.5 %all-gather.15.cloned.1.call-done = bf16[2,1024,1024]{2,1,0:T(8,128)(2,1)} async-done(((bf16[2,128,1024]{2,1,0:T(8,128)(2,1)}), bf16[2,1024,1024]{2,1,0:T(8,128)(2,1)}) %all-gather.15.cloned.1.call-update) | async-done | bytes 4194320 | tf_op jit(solution)/shard_map/all_gather | solution.py:135
  241.2 68.1 %all-gather.19.cloned.1.call-done = bf16[2,1024,1024]{2,1,0:T(8,128)(2,1)} async-done(((bf16[2,128,1024]{2,1,0:T(8,128)(2,1)}), bf16[2,1024,1024]{2,1,0:T(8,128)(2,1)}) %all-gather.19.cloned.1.call-update) | async-done | bytes 4194320 | tf_op jit(solution)/shard_map/all_gather | solution.py:134
  315.5 82.1 %while.68 = (s32[]{:T(128)}, f32[2,16,128]{2,1,0:T(8,128)S(1)}, f32[2,16,128]{2,1,0:T(8,128)S(1)}, s32[2]{0:T(128)S(1)}, s32[2]{0:T(128)S(1)}, /*index=5*/bf16[2...) while((s32[]{:T(128)}, f32[2,16,128]{2,1,0:T(8,128)S(1)}, ...), condition=%wide.region_4.5_spmd.clone, body=%wide.region_1.4_spmd.clone.sunk | while | flops 287342080 | bytes 81746984 | solution.py:175
  397.6 67.2 %while.69 = (s32[]{:T(128)}, f32[2,128,16,64]{1,3,2,0:T(8,128)S(1)}, s32[2]{0:T(128)S(1)}, bf16[2,1024,16,64]{1,3,2,0:T(8,128)(2,1)}, s32[2]{0:T(128)S(1)}, /*in...) while((s32[]{:T(128)}, ...), condition=%wide.region_6.7_spmd.clone, body=%wide.region_5.6_spmd.clone.sunk | while | flops 547892736 | bytes 64773676 | solution.py:191
  475.1 326.0 %all-gather.25.cloned.1.call-done = bf16[4,2816,1024]{2,1,0:T(8,128)(2,1)} async-done(((bf16[4,352,1024]{2,1,0:T(8,128)(2,1)}), bf16[4,2816,1024]{2,1,0:T(8,128)(2,1)}) %all-gather.25.cloned.1.call-update) | async-done | bytes 23068688 | tf_op jit(solution)/shard_map/all_gather | solution.py:228
  801.2 14.0 fusion.119
  815.2 428.6 %all-gather.27.cloned.1.call-done = bf16[4,2816,1024]{2,1,0:T(8,128)(2,1)} async-done(((bf16[4,352,1024]{2,1,0:T(8,128)(2,1)}), bf16[4,2816,1024]{2,1,0:T(8,128)(2,1)}) %all-gather.27.cloned.1.call-update) | async-done | bytes 23068688 | tf_op jit(solution)/shard_map/all_gather | solution.py:229
  1243.8 24.4 multiply_convert_fusion.1
  1268.2 418.3 %all-gather.29.cloned.1.call-done = bf16[4,2816,1024]{2,1,0:T(8,128)(2,1)} async-done(((bf16[4,352,1024]{2,1,0:T(8,128)(2,1)}), bf16[4,2816,1024]{2,1,0:T(8,128)(2,1)}) %all-gather.29.cloned.1.call-update) | async-done | bytes 23068688 | tf_op jit(solution)/shard_map/all_gather | solution.py:230
  1711.8 20.7 multiply_convert_fusion
  1787.1 79.8 %while.70 = (s32[]{:T(128)}, f32[2,16,128]{2,1,0:T(8,128)S(1)}, s32[2]{0:T(128)S(1)}, s32[2]{0:T(128)S(1)}, bf16[2,1024,16,64]{1,3,2,0:T(8,128)(2,1)}, /*index=5...) while((s32[]{:T(128)}, f32[2,16,128]{2,1,0:T(8,128)S(1)}, ...), condition=%wide.region_27.29_spmd.clone, body=%wide.region_25.28_spmd.clone.sunk | while | flops 549469696 | bytes 80042040 | solution.py:323
  1867.0 205.1 %while.71 = (s32[]{:T(128)}, f32[2,128,16,64]{1,3,2,0:T(8,128)S(1)}, f32[32,16]{0,1:T(8,128)S(1)}, bf16[2,512,2,1024]{3,1,0,2:T(8,128)(2,1)}, bf16[2,512,2,1024]...) while((s32[]{:T(128)}, ...), condition=%wide.region_31.33_spmd.clone, body=%wide.region_28.32_spmd.clone.sunk | while | flops 1376532992 | bytes 282455744 | solution.py:371
  1927.9 15.0 dynamic-update-slice.7
  2030.1 15.0 dynamic-update-slice.7
  2079.5 80.9 %reduce-scatter.13.cloned.1.call-done = bf16[128,2,1024]{2,0,1:T(8,128)(2,1)} async-done(((bf16[1024,2,1024]{2,0,1:T(8,128)(2,1)}), bf16[128,2,1024]{2,0,1:T(8,128)(2,1)}) %reduce-scatter.13.cloned.1.call-update) | async-done | bytes 524304 | tf_op jit(solution)/shard_map/reduce_scatter | solution.py:373
  2163.6 88.7 %reduce-scatter.15.cloned.1.call-done = bf16[128,2,1024]{2,0,1:T(8,128)(2,1)} async-done(((bf16[1024,2,1024]{2,0,1:T(8,128)(2,1)}), bf16[128,2,1024]{2,0,1:T(8,128)(2,1)}) %reduce-scatter.15.cloned.1.call-update) | async-done | bytes 524304 | tf_op jit(solution)/shard_map/reduce_scatter | solution.py:379
  2282.6 13.7 convolution_convert_fusion
  2298.5 23.8 reduce-scatter.17.cloned.1.call-done
  2322.2 70.1 %reduce-scatter.23.cloned.1.call-done = bf16[128,1024]{1,0:T(8,128)(2,1)} async-done(((bf16[1024,1024]{1,0:T(8,128)(2,1)}), bf16[128,1024]{1,0:T(8,128)(2,1)}) %reduce-scatter.23.cloned.1.call-update) | async-done | bytes 262160 | tf_op jit(solution)/shard_map/reduce_scatter | solution.py:437
  2392.3 70.7 %reduce-scatter.19.cloned.1.call-done = bf16[128,1024]{1,0:T(8,128)(2,1)} async-done(((bf16[1024,1024]{1,0:T(8,128)(2,1)}), bf16[128,1024]{1,0:T(8,128)(2,1)}) %reduce-scatter.19.cloned.1.call-update) | async-done | bytes 262160 | tf_op jit(solution)/shard_map/reduce_scatter | solution.py:431
  2463.1 70.6 %reduce-scatter.21.cloned.1.call-done = bf16[128,1024]{1,0:T(8,128)(2,1)} async-done(((bf16[1024,1024]{1,0:T(8,128)(2,1)}), bf16[128,1024]{1,0:T(8,128)(2,1)}) %reduce-scatter.21.cloned.1.call-update) | async-done | bytes 262160 | tf_op jit(solution)/shard_map/reduce_scatter | solution.py:434
  2533.7 378.2 %reduce-scatter.25.cloned.1.call-done = bf16[4,352,1024]{2,1,0:T(8,128)(2,1)} async-done(((bf16[4,2816,1024]{2,1,0:T(8,128)(2,1)}), bf16[4,352,1024]{2,1,0:T(8,128)(2,1)}) %reduce-scatter.25.cloned.1.call-update) | async-done | bytes 2883600 | tf_op jit(solution)/shard_map/reduce_scatter | solution.py:287
  2911.9 376.5 %reduce-scatter.27.cloned.1.call-done = bf16[4,352,1024]{2,1,0:T(8,128)(2,1)} async-done(((bf16[4,2816,1024]{2,1,0:T(8,128)(2,1)}), bf16[4,352,1024]{2,1,0:T(8,128)(2,1)}) %reduce-scatter.27.cloned.1.call-update) | async-done | bytes 2883600 | tf_op jit(solution)/shard_map/reduce_scatter | solution.py:290
  3288.4 376.4 %reduce-scatter.29.cloned.1.call-done = bf16[4,352,1024]{2,1,0:T(8,128)(2,1)} async-done(((bf16[4,2816,1024]{2,1,0:T(8,128)(2,1)}), bf16[4,352,1024]{2,1,0:T(8,128)(2,1)}) %reduce-scatter.29.cloned.1.call-update) | async-done | bytes 2883600 | tf_op jit(solution)/shard_map/reduce_scatter | solution.py:293
  3667.4 59.8 %reduce-scatter.31.cloned.1.call-done = bf16[128,4]{1,0:T(8,128)(2,1)} async-done(((bf16[1024,4]{1,0:T(8,128)(2,1)}), bf16[128,4]{1,0:T(8,128)(2,1)}) %reduce-scatter.31.cloned.1.call-update) | async-done | bytes 1040
  3736.4 16.2 all-reduce.10
  3768.8 138.6 %all-reduce.15.cloned.1.call-done = (bf16[128,1024]{1,0:T(8,128)(2,1)}, bf16[128,1024]{1,0:T(8,128)(2,1)}, bf16[128,1024]{1,0:T(8,128)(2,1)}, bf16[128,1024]{1,0...) async-done(((bf16[128,1024]{1,0:T(8,128)(2,1)}, bf16[128,1024]{1,0:T(8,128)(2,1)}, ...) | async-done | bytes 9699344 | tf_op jit(solution)/shard_map/psum | solution.py:464
  (538 shorter events, 637.0 us)
Async XLA Ops:
  7.2 53.3 %all-gather.13.cloned.1.call-start = ((), (), s32[]{:S(2)}) async-start(), calls=%async_computation.10 | async-start | bytes 2359296 | tf_op jit(solution)/shard_map/all_gather | solution.py:108
  7.9 102.5 %all-gather.17.cloned.1.call-start = ((), (), s32[]{:S(2)}) async-start(), calls=%async_computation.12 | async-start | bytes 2359296 | tf_op jit(solution)/shard_map/all_gather | solution.py:107
  8.7 171.9 %all-gather.21.cloned.1.call-start = ((), (), s32[]{:S(2)}) async-start(), calls=%async_computation.14 | async-start | bytes 2359296 | tf_op jit(solution)/shard_map/all_gather | solution.py:106
  9.4 225.6 %all-gather.15.cloned.1.call-start = ((), (), s32[]{:S(2)}) async-start(), calls=%async_computation.11 | async-start | bytes 4718592 | tf_op jit(solution)/shard_map/all_gather | solution.py:135
  31.0 83.8 %copy-start.30 = (bf16[256,1024]{1,0:T(8,128)(2,1)}, bf16[256,1024]{1,0:T(8,128)(2,1)S(1)}, u32[]{:S(2)}) copy-start(bf16[256,1024]{1,0:T(8,128)(2,1)S(1)} %fusion.102) | copy-start | bytes 1572868
  63.6 245.7 %all-gather.19.cloned.1.call-start = ((), (), s32[]{:S(2)}) async-start(), calls=%async_computation.13 | async-start | bytes 4718592 | tf_op jit(solution)/shard_map/all_gather | solution.py:134
  113.5 352.6 %all-gather.23.cloned.1.call-start = ((), (), s32[]{:S(2)}) async-start(), calls=%async_computation.15 | async-start | bytes 2359296 | tf_op jit(solution)/shard_map/all_gather | solution.py:109
  114.1 687.1 %all-gather.25.cloned.1.call-start = ((), (), s32[]{:S(2)}) async-start(), calls=%async_computation.16 | async-start | bytes 25952256 | tf_op jit(solution)/shard_map/all_gather | solution.py:228
  114.9 1128.9 %all-gather.27.cloned.1.call-start = ((), (), s32[]{:S(2)}) async-start(), calls=%async_computation.17 | async-start | bytes 25952256 | tf_op jit(solution)/shard_map/all_gather | solution.py:229
  115.6 1570.9 %all-gather.29.cloned.1.call-start = ((), (), s32[]{:S(2)}) async-start(), calls=%async_computation.18 | async-start | bytes 25952256 | tf_op jit(solution)/shard_map/all_gather | solution.py:230
  116.4 2044.0 %reduce-scatter.13.cloned.1.call-start = ((), (), s32[]{:S(2)}) async-start(), calls=%async_computation.19 | async-start | bytes 4718592 | tf_op jit(solution)/shard_map/reduce_scatter | solution.py:373
  315.5 82.1 %copy-start.29 = (f32[2,128,16,64]{1,3,2,0:T(8,128)S(1)}, f32[2,128,16,64]{1,3,2,0:T(8,128)}, u32[]{:S(2)}) copy-start(f32[2,128,16,64]{1,3,2,0:T(8,128)} %custom-call.2) | copy-start | bytes 3145732
  469.9 331.2 %copy-start.32 = (bf16[4,160]{1,0:T(4,128)(2,1)S(1)}, bf16[4,160]{1,0:T(4,128)(2,1)}, u32[]{:S(2)}) copy-start(bf16[4,160]{1,0:T(4,128)(2,1)} %convert_element_type.267) | copy-start | bytes 3844
  470.0 331.2 %copy-start.34 = (pred[4,160]{1,0:T(4,128)(4,1)S(1)}, pred[4,160]{1,0:T(4,128)(4,1)}, u32[]{:S(2)}) copy-start(pred[4,160]{1,0:T(4,128)(4,1)} %compare_and_fusion) | copy-start | bytes 1924
  472.8 771.0 %copy-start.9 = (bf16[640,1024]{1,0:T(8,128)(2,1)}, bf16[640,1024]{1,0:T(8,128)(2,1)S(1)}, u32[]{:S(2)}) copy-start(bf16[640,1024]{1,0:T(8,128)(2,1)S(1)} %gather_fusion) | copy-start | bytes 3932164
  473.8 1298.1 %copy-start.39 = (f32[256,4]{0,1:T(4,128)}, f32[256,4]{0,1:T(4,128)S(1)}, u32[]{:S(2)}) copy-start(f32[256,4]{0,1:T(4,128)S(1)} %get-tuple-element.1486) | copy-start | bytes 12292
  474.4 1297.5 %copy-start.58 = (f32[256]{0:T(256)}, f32[256]{0:T(256)S(1)}, u32[]{:S(2)}) copy-start(f32[256]{0:T(256)S(1)} %fusion.126) | copy-start | bytes 3076
  1787.0 79.9 %copy-start.6 = (f32[2,128,16,64]{1,3,2,0:T(8,128)S(1)}, f32[2,128,16,64]{1,3,2,0:T(8,128)}, u32[]{:S(2)}) copy-start(f32[2,128,16,64]{1,3,2,0:T(8,128)} %custom-call.4) | copy-start | bytes 3145732
  1787.0 79.9 %copy-start.50 = (s32[2047]{0:T(1024)S(1)}, s32[2047]{0:T(1024)}, u32[]{:S(2)}) copy-start(s32[2047]{0:T(1024)} %param.29) | copy-start | bytes 24568
  2072.1 180.2 %reduce-scatter.15.cloned.1.call-start = ((), (), s32[]{:S(2)}) async-start(), calls=%async_computation.20 | async-start | bytes 4718592 | tf_op jit(solution)/shard_map/reduce_scatter | solution.py:379
  2072.9 249.4 %reduce-scatter.17.cloned.1.call-start = ((), (), s32[]{:S(2)}) async-start(), calls=%async_computation.21 | async-start | bytes 2359296 | tf_op jit(solution)/shard_map/reduce_scatter | solution.py:428
  2076.1 316.2 %reduce-scatter.23.cloned.1.call-start = ((), (), s32[]{:S(2)}) async-start(), calls=%async_computation.24 | async-start | bytes 2359296 | tf_op jit(solution)/shard_map/reduce_scatter | solution.py:437
  2079.4 383.6 %reduce-scatter.19.cloned.1.call-start = ((), (), s32[]{:S(2)}) async-start(), calls=%async_computation.22 | async-start | bytes 2359296 | tf_op jit(solution)/shard_map/reduce_scatter | solution.py:431
  2163.5 92.0 %copy-start.10 = (bf16[640,1024]{1,0:T(8,128)(2,1)S(1)}, bf16[640,1024]{1,0:T(8,128)(2,1)}, u32[]{:S(2)}) copy-start(bf16[640,1024]{1,0:T(8,128)(2,1)} %copy-done.9) | copy-start | bytes 3932164
  2163.5 92.0 %copy-start.33 = (bf16[4,160]{1,0:T(4,128)(2,1)S(1)}, bf16[4,160]{1,0:T(4,128)(2,1)}, u32[]{:S(2)}) copy-start(bf16[4,160]{1,0:T(4,128)(2,1)} %convert_element_type.267) | copy-start | bytes 3844
  2163.5 92.0 %copy-start.35 = (pred[4,160]{1,0:T(4,128)(4,1)S(1)}, pred[4,160]{1,0:T(4,128)(4,1)}, u32[]{:S(2)}) copy-start(pred[4,160]{1,0:T(4,128)(4,1)} %compare_and_fusion) | copy-start | bytes 1924
  2163.5 370.2 %reduce-scatter.21.cloned.1.call-start = ((), (), s32[]{:S(2)}) async-start(), calls=%async_computation.23 | async-start | bytes 2359296 | tf_op jit(solution)/shard_map/reduce_scatter | solution.py:434
  2255.4 656.5 %reduce-scatter.25.cloned.1.call-start = ((), (), s32[]{:S(2)}) async-start(), calls=%async_computation.25 | async-start | bytes 25952256 | tf_op jit(solution)/shard_map/reduce_scatter | solution.py:287
  2268.6 1019.8 %reduce-scatter.27.cloned.1.call-start = ((), (), s32[]{:S(2)}) async-start(), calls=%async_computation.26 | async-start | bytes 25952256 | tf_op jit(solution)/shard_map/reduce_scatter | solution.py:290
  2281.9 1382.9 %reduce-scatter.29.cloned.1.call-start = ((), (), s32[]{:S(2)}) async-start(), calls=%async_computation.27 | async-start | bytes 25952256 | tf_op jit(solution)/shard_map/reduce_scatter | solution.py:293
  2296.3 1430.8 %reduce-scatter.31.cloned.1.call-start = ((), (), s32[]{:S(2)}) async-start(), calls=%async_computation.28 | async-start | bytes 294912
  2298.4 1608.9 %all-reduce.15.cloned.1.call-start = ((), (), s32[]{:S(2)}) async-start(), calls=%async_computation.29 | async-start | bytes 19398656 | tf_op jit(solution)/shard_map/psum | solution.py:464
  (80 other events, 789.1 us)
Sparse Core Ops, SparseCore 0:
  10.1 50.2 all-gather.12
  62.6 47.7 all-gather.16
  112.5 47.8 all-gather.20
  163.0 71.8 all-gather.14
  237.6 71.6 all-gather.18
  311.2 47.6 all-gather.22
  360.4 440.6 all-gather.24
  802.7 441.0 all-gather.26
  1245.4 441.0 all-gather.28
  2072.3 88.0 reduce-scatter.12
  2164.5 87.7 reduce-scatter.14
  2256.3 65.9 reduce-scatter.16
  2325.8 66.5 reduce-scatter.22
  2396.3 66.7 reduce-scatter.18
  2467.0 66.6 reduce-scatter.20
  2537.4 374.4 reduce-scatter.24
  2915.6 372.7 reduce-scatter.26
  3292.1 372.6 reduce-scatter.28
  3668.7 58.3 reduce-scatter.30
  3730.3 177.0 all-reduce.14
where the time goes:
time: 3940 us; the launch traced here: 3930 us
  waiting for transfers between devices  3110 us (79%)
  local copies, waits for them, and re-layouts  373 us (9%)
  matrix products  274 us (7%)
  blocking collectives  89.1 us (2%)
  other arithmetic  62.4 us (2%)
    all_gather x1, waiting for transfers between devices, body(): up_piece = lax.all_gather(w_up, 'shard', axis=1, tiled=True)  429 us
    all_gather x1, waiting for transfers between devices, body(): down_piece = lax.all_gather(w_down, 'shard', axis=1, tiled=True)  418 us
    reduce_scatter x1, waiting for transfers between devices, body(): lax.psum_scatter(full_gate.astype(jnp.bfloat16), 'shard', scatter_dimensi...  378 us
    reduce_scatter x1, waiting for transfers between devices, body(): lax.psum_scatter(full_up.astype(jnp.bfloat16), 'shard', scatter_dimension...  377 us
    reduce_scatter x1, waiting for transfers between devices, body(): lax.psum_scatter(full_down.astype(jnp.bfloat16), 'shard', scatter_dimensi...  376 us
    all_gather x1, waiting for transfers between devices, body(): gate_piece = lax.all_gather(w_gate, 'shard', axis=1, tiled=True)  326 us
    psum x1, waiting for transfers between devices, body(): lax.psum(share_query.astype(jnp.bfloat16), 'rep').astype(jnp.float32)  139 us
    reduce_scatter x1, waiting for transfers between devices, body(): lax.psum_scatter(value_parts.reshape(seq_len, seq_count, width).astype(jn...  88.7 us
  transfers between devices with their start and end apart: 20, of which 18 were waited for; matrix products, arithmetic and copies ran while one was open for 8% of the time, Pallas kernels for 0%

commit v1 on v0

v1 whole, which is shorter than its diff:
```python
import functools

import jax
import jax.numpy as jnp
from jax import lax
from jax.experimental import pallas as pl
from jax.experimental.pallas import tpu as pltpu
from jax.sharding import PartitionSpec as P

epsilon = 1e-06
highest = lax.Precision.HIGHEST
bf16 = jnp.bfloat16
f32 = jnp.float32
vmem_limit = 58 * 1024 * 1024
whole_ref = pl.BlockSpec(memory_space=pltpu.VMEM)


def dot_nt(left, right):
    return lax.dot_general(left, right, (((1,), (1,)), ((), ())), preferred_element_type=f32)


def dot_tn(left, right):
    return lax.dot_general(left, right, (((0,), (0,)), ((), ())), preferred_element_type=f32)


def dot_nn(left, right):
    return lax.dot_general(left, right, (((1,), (0,)), ((), ())), preferred_element_type=f32)


def ring_index(place, count):
    return jnp.where(place < count // 2, 2 * place, 2 * count - 1 - 2 * place)


def ring_place(index, count):
    return jnp.where(index % 2 == 0, index // 2, count - 1 - index // 2)


def ring_send(value, step, count):
    order = [2 * i if i < count // 2 else 2 * count - 1 - 2 * i for i in range(count)]
    pairs = [(order[i], order[(i + step) % count]) for i in range(count)]
    return lax.ppermute(value, "shard", pairs)


def ring_gather(value, count):
    half = value.shape[0] // 2
    ahead = behind = value
    pieces = [(0, 0, value)]
    for step in range(1, count // 2):
        behind = ring_send(behind, 1, count)
        ahead = ring_send(ahead, -1, count)
        pieces += [(count - step, 0, behind), (step, 0, ahead)]
    far = count // 2
    pieces.append((far, 0, ring_send(behind[:half], 1, count)))
    pieces.append((far, half, ring_send(ahead[half:], -1, count)))
    return pieces


def pieces_in_order(pieces, count):
    out = [None] * count
    for distance, first, piece in pieces:
        if out[distance] is None:
            out[distance] = piece
        else:
            out[distance] = jnp.concatenate([out[distance], piece], axis=0)
    return out


def add_low(left, right):
    return (left.astype(f32) + right.astype(f32)).astype(bf16)


def ring_sum(chunk_of, count):
    far = chunk_of(count // 2)
    half = far.shape[0] // 2
    right = ring_send(far[:half], 1, count)
    left = ring_send(far[half:], -1, count)
    for step in range(count // 2 - 1, 0, -1):
        own_right, own_left = chunk_of(step), chunk_of(count - step)
        if right.shape[0] == half:
            right = jnp.concatenate([add_low(right, own_right[:half]), own_right[half:]], axis=0)
            left = jnp.concatenate([own_left[:half], add_low(left, own_left[half:])], axis=0)
        else:
            right = add_low(right, own_right)
            left = add_low(left, own_left)
        right = ring_send(right, 1, count)
        left = ring_send(left, -1, count)
    return right, left


def swap(value, axis, count, bit):
    return lax.ppermute(value, axis, [(i, i ^ bit) for i in range(count)])


def bits_of(count):
    return [1 << i for i in range(count.bit_length() - 1)]


def rep_scatter(value, count, me):
    for bit in bits_of(count):
        value = value.reshape((value.shape[0] // 2, 2) + value.shape[1:])
        side = (me // bit) % 2
        sent = lax.dynamic_index_in_dim(value, 1 - side, 1, keepdims=False)
        kept = lax.dynamic_index_in_dim(value, side, 1, keepdims=False)
        value = add_low(kept, swap(sent, "rep", count, bit))
    return value[0]


def rep_gather(value, count, me):
    value = value[None]
    for bit in bits_of(count)[::-1]:
        other = swap(value, "rep", count, bit)
        side = (me // bit) % 2
        low = jnp.where(side == 0, value, other)
        high = jnp.where(side == 0, other, value)
        value = jnp.stack([low, high], axis=1).reshape((2 * value.shape[0],) + value.shape[1:])
    return value


def rep_total(value, count, me):
    value = value.reshape((2, value.shape[0] // 2) + value.shape[1:])
    side = me % 2
    sent = lax.dynamic_index_in_dim(value, 1 - side, 0, keepdims=False)
    kept = lax.dynamic_index_in_dim(value, side, 0, keepdims=False)
    mine = add_low(kept, swap(sent, "rep", count, 1))
    for bit in bits_of(count)[1:]:
        mine = add_low(mine, swap(mine, "rep", count, bit))
    other = swap(mine, "rep", count, 1)
    low = jnp.where(side == 0, mine, other)
    high = jnp.where(side == 0, other, mine)
    return jnp.concatenate([low, high], axis=0).astype(f32)


def assign_slots(pair_ids, alive_pairs, expert_count, capacity):
    expert_range = jnp.arange(expert_count, dtype=jnp.int32)
    hit_table = (pair_ids[:, None] == expert_range[None, :]).astype(jnp.int32) * alive_pairs[
        :, None
    ]
    earlier = jnp.cumsum(hit_table, axis=0, dtype=jnp.int32) - hit_table
    placing = jnp.sum(earlier * hit_table, axis=1, dtype=jnp.int32)
    return jnp.logical_and(alive_pairs > 0, placing < capacity)


def toeplitz_rows(window, row_count, col_count):
    lead = window.shape[:-1]
    padded = jnp.concatenate([window, jnp.zeros(lead + (1,), window.dtype)], axis=-1)
    rolled = jnp.concatenate([padded[..., row_count - 1 :], padded[..., : row_count - 1]], axis=-1)
    period = row_count + col_count
    tiled = jnp.tile(rolled, (1,) * len(lead) + (row_count,))
    shaped = tiled[..., : row_count * (period - 1)].reshape(lead + (row_count, period - 1))
    return shaped[..., :col_count]


def diagonal_sums(table, row_count, col_count):
    lead = table.shape[:-2]
    period = row_count + col_count
    widened = jnp.concatenate(
        [table, jnp.zeros(lead + (row_count, row_count - 1), table.dtype)], axis=-1
    )
    flat = widened.reshape(lead + (row_count * (period - 1),))
    flat = jnp.concatenate(
        [
            jnp.zeros(lead + (row_count - 1,), table.dtype),
            flat,
            jnp.zeros(lead + (1,), table.dtype),
        ],
        axis=-1,
    )
    shaped = flat.reshape(lead + (row_count, period))
    return jnp.sum(shaped[..., : period - 1], axis=-2)


def attend_kernel(places, span, heads, head_size, meta, *refs):
    pieces, (weight, bias, tokens_out, qkv_out, context_out) = refs[: len(places)], refs[len(places) :]
    length = meta[0]
    seq_len = tokens_out.shape[0]
    blocks = seq_len // 128
    for (distance, first), piece in zip(places, pieces):
        rows = min(span - first, piece.shape[0])
        low = piece[0:rows, :]
        wide = low.astype(f32)
        factor = lax.rsqrt(jnp.mean(wide * wide, axis=-1, keepdims=True) + epsilon)
        made = dot_nn(low, weight[...]) * factor
        start = pl.multiple_of(meta[1 + distance] * span + first, 16)
        tokens_out[pl.ds(start, rows), :] = low
        for part in range(3 * heads):
            cut = made[:, part * head_size : (part + 1) * head_size]
            if part < heads:
                cut = cut.astype(bf16).astype(f32) * head_size ** (-0.5)
            qkv_out[part, pl.ds(start, rows), :] = cut.astype(bf16)
    for head in range(heads):
        keys = qkv_out[heads + head]
        values = qkv_out[2 * heads + head]
        for block in range(0, blocks, 2):
            queries = qkv_out[head, block * 128 : block * 128 + 256, :]
            scores = dot_nt(queries, keys)
            first_col = (blocks - 1 - block) * 128
            added = jnp.concatenate(
                [
                    bias[head, :, first_col : first_col + seq_len],
                    bias[head, :, first_col - 128 : first_col - 128 + seq_len],
                ],
                axis=0,
            )
            column = lax.broadcasted_iota(jnp.int32, scores.shape, 1)
            scores = jnp.where(column < length, scores + added, -1e30)
            top = jnp.max(scores, axis=-1, keepdims=True)
            weights = jnp.exp(scores - top)
            total = jnp.sum(weights, axis=-1, keepdims=True)
            mixed = dot_nn(weights.astype(bf16), values) / total
            context_out[
                block * 128 : block * 128 + 256, head * head_size : (head + 1) * head_size
            ] = mixed.astype(bf16)


def attend(meta, pieces, weight, bias, span, heads, head_size):
    width = weight.shape[0]
    seq_len = span * (meta.shape[0] - 2)
    places = [(distance, first) for distance, first, piece in pieces]
    return pl.pallas_call(
        functools.partial(attend_kernel, places, span, heads, head_size),
        out_shape=(
            jax.ShapeDtypeStruct((seq_len, width), bf16),
            jax.ShapeDtypeStruct((3 * heads, seq_len, head_size), bf16),
            jax.ShapeDtypeStruct((seq_len, heads * head_size), bf16),
        ),
        grid_spec=pltpu.PrefetchScalarGridSpec(
            num_scalar_prefetch=1,
            grid=(),
            in_specs=[whole_ref] * (len(pieces) + 2),
            out_specs=[whole_ref] * 3,
        ),
        compiler_params=pltpu.CompilerParams(vmem_limit_bytes=vmem_limit),
        cost_estimate=pl.CostEstimate(
            flops=20 * 10**9, bytes_accessed=8 * 10**6, transcendentals=heads * seq_len * seq_len
        ),
        name="attend",
    )(meta, *[piece for distance, first, piece in pieces], weight, bias)


def experts_kernel(count, span, expert_count, meta, tokens, *refs):
    context = refs[:count]
    (
        out_weight,
        gain,
        router_weight,
        codes,
        cotangent,
        gate_weight,
        up_weight,
        down_weight,
        context_out,
        normed_out,
        hidden_out,
        grad_gate_out,
        grad_up_out,
        mix_out,
        grad_out,
        heads_out,
        logits_out,
        gain_out,
    ) = refs[count:]
    rows, width = tokens.shape
    step = pl.program_id(0)
    length, me = meta[0], meta[meta.shape[0] - 1]
    row = step * rows + lax.broadcasted_iota(jnp.int32, (rows, 1), 0)
    own = jnp.logical_and(row >= me * span, row < (me + 1) * span)
    joined = jnp.concatenate([piece[...] for piece in context], axis=1)
    context_out[...] = joined
    hidden = tokens[...].astype(f32) + dot_nn(joined, out_weight[...])
    factor = lax.rsqrt(jnp.mean(hidden * hidden, axis=-1, keepdims=True) + epsilon)
    normed = (hidden * factor * gain[...]).astype(bf16)
    normed_out[...] = normed
    logits = dot_nn(normed, router_weight[...])
    lane = lax.broadcasted_iota(jnp.int32, logits.shape, 1)
    logits = jnp.where(lane < expert_count, logits, -1e30)
    router = jnp.exp(logits - jnp.max(logits, axis=-1, keepdims=True))
    router = router / jnp.sum(router, axis=-1, keepdims=True)
    code = codes[...]
    chosen = (code > 0.5).astype(f32)
    kept = (code > 1.5).astype(f32)
    pair_total = jnp.sum(router * chosen, axis=-1, keepdims=True)
    share = router * chosen / pair_total
    scale = share * kept
    upstream = jnp.where(row < length, cotangent[...].astype(f32), 0.0)
    upstream_low = upstream.astype(bf16)
    chunks, _, chunk = hidden_out.shape
    units = chunk * chunks // expert_count
    mix = jnp.zeros((rows, width), f32)
    grad = jnp.zeros((rows, width), f32)
    pair_grads = jnp.zeros(logits.shape, f32)
    column = lax.broadcasted_iota(jnp.int32, (rows, chunk), 1)
    root = 0.7978845608028654
    for part in range(chunks):
        cut = slice(part * chunk, (part + 1) * chunk)
        gate_in = dot_nt(normed, gate_weight[cut, :])
        up_in = dot_nt(normed, up_weight[cut, :])
        grad_hidden = dot_nt(upstream_low, down_weight[cut, :])
        square = gate_in * gate_in
        curve = jnp.tanh(root * gate_in * (1.0 + 0.044715 * square))
        rise = 0.5 + 0.5 * curve
        gelu = gate_in * rise
        slope = rise + 0.5 * gate_in * (1.0 - curve * curve) * (
            root + (3 * 0.044715 * root) * square
        )
        hidden_unit = gelu * up_in
        product = hidden_unit * grad_hidden
        per_chunk = chunk // units
        scales = scale[:, part * per_chunk : part * per_chunk + 1]
        for member in range(1, per_chunk):
            expert = part * per_chunk + member
            scales = jnp.where(column < member * units, scales, scale[:, expert : expert + 1])
        for member in range(per_chunk):
            expert = part * per_chunk + member
            inside = jnp.logical_and(column >= member * units, column < (member + 1) * units)
            pair_sum = jnp.sum(jnp.where(inside, product, 0.0), axis=-1, keepdims=True)
            pair_grads = jnp.where(lane == expert, pair_sum, pair_grads)
        scaled_grad = scales * grad_hidden
        hidden_low = (scales * hidden_unit).astype(bf16)
        grad_gate = (scaled_grad * up_in * slope).astype(bf16)
        grad_up = (scaled_grad * gelu).astype(bf16)
        hidden_out[part] = hidden_low
        grad_gate_out[part] = grad_gate
        grad_up_out[part] = grad_up
        mix = mix + dot_nn(hidden_low, down_weight[cut, :])
        grad = grad + dot_nn(grad_gate, gate_weight[cut, :])
        grad = grad + dot_nn(grad_up, up_weight[cut, :])
    mix_out[...] = (mix + jnp.where(own, hidden, 0.0)).astype(bf16)
    pair_grads = pair_grads * kept
    weighted = jnp.sum(pair_grads * share, axis=-1, keepdims=True)
    grad_router = chosen * (pair_grads - weighted) / pair_total
    grad_logits = router * (grad_router - jnp.sum(router * grad_router, axis=-1, keepdims=True))
    grad_logits = grad_logits.astype(bf16)
    logits_out[...] = grad_logits
    grad = grad + dot_nt(grad_logits, router_weight[...])
    spread = hidden * factor
    gain_part = jnp.sum(grad * spread, axis=0, keepdims=True)

    @pl.when(step == 0)
    def _():
        gain_out[...] = jnp.zeros_like(gain_out)

    gain_out[0:1, :] += gain_part
    grad = grad * gain[...]
    middle = jnp.mean(grad * hidden, axis=-1, keepdims=True) * (factor * factor)
    back = factor * grad - spread * middle + jnp.where(own, upstream, 0.0)
    back = back.astype(bf16)
    grad_out[...] = back
    grad_heads = dot_nt(back, out_weight[...]).astype(bf16)
    each = width // count
    for place in range(count):
        heads_out[place] = grad_heads[:, place * each : (place + 1) * each]


def experts(
    meta, tokens, context, out_weight, gain, router_weight, codes, cotangent, weights, span, expert_count
):
    seq_len, width = tokens.shape
    count = len(context)
    units = weights[0].shape[0]
    chunks = expert_count // 2
    chunk = units // chunks
    rows = 256
    by_row = lambda cols: pl.BlockSpec((rows, cols), lambda i, meta: (i, 0))
    fixed = lambda shape: pl.BlockSpec(
        shape, lambda i, meta: (0,) * len(shape), pipeline_mode=pl.Buffered(1)
    )
    by_chunk = pl.BlockSpec((chunks, rows, chunk), lambda i, meta: (0, i, 0))
    each = width // count
    low = lambda *shape: jax.ShapeDtypeStruct(shape, bf16)
    return pl.pallas_call(
        functools.partial(experts_kernel, count, span, expert_count),
        out_shape=(
            low(seq_len, width),
            low(seq_len, width),
            low(chunks, seq_len, chunk),
            low(chunks, seq_len, chunk),
            low(chunks, seq_len, chunk),
            low(seq_len, width),
            low(seq_len, width),
            low(count, seq_len, each),
            low(seq_len, 128),
            jax.ShapeDtypeStruct((8, width), f32),
        ),
        grid_spec=pltpu.PrefetchScalarGridSpec(
            num_scalar_prefetch=1,
            grid=(seq_len // rows,),
            in_specs=[by_row(width)]
            + [by_row(each)] * count
            + [
                fixed(out_weight.shape),
                fixed(gain.shape),
                fixed(router_weight.shape),
                by_row(128),
                by_row(width),
            ]
            + [fixed(weight.shape) for weight in weights],
            out_specs=(
                by_row(width),
                by_row(width),
                by_chunk,
                by_chunk,
                by_chunk,
                by_row(width),
                by_row(width),
                pl.BlockSpec((count, rows, each), lambda i, meta: (0, i, 0)),
                by_row(128),
                pl.BlockSpec((8, width), lambda i, meta: (0, 0)),
            ),
        ),
        compiler_params=pltpu.CompilerParams(vmem_limit_bytes=vmem_limit),
        cost_estimate=pl.CostEstimate(
            flops=2 * seq_len * width * (6 * units + 2 * width),
            bytes_accessed=40 * 10**6,
            transcendentals=seq_len * units,
        ),
        name="experts",
    )(meta, tokens, *context, out_weight, gain, router_weight, codes, cotangent, *weights)


def attend_back_kernel(
    heads,
    head_size,
    meta,
    tokens,
    qkv,
    grad_heads,
    weight,
    bias,
    grad_in,
    grad_out,
    parts_out,
    bias_out,
    gain_out,
    key_sum,
    value_sum,
    joined,
):
    length = meta[0]
    seq_len = tokens.shape[0]
    blocks = seq_len // 128
    width_heads = heads * head_size
    bias_out[...] = jnp.zeros_like(bias_out)
    for head in range(heads):
        keys = qkv[heads + head]
        values = qkv[2 * heads + head]
        lanes = slice(head * head_size, (head + 1) * head_size)
        for block in range(0, blocks, 2):
            span = slice(block * 128, block * 128 + 256)
            queries = qkv[head, span, :]
            grads = grad_heads[span, lanes]
            first_row = (blocks - 1 - block) * 128
            added = jnp.concatenate(
                [
                    bias[head, first_row : first_row + seq_len, :],
                    bias[head, first_row - 128 : first_row - 128 + seq_len, :],
                ],
                axis=1,
            )
            scores = dot_nt(keys, queries)
            row = lax.broadcasted_iota(jnp.int32, scores.shape, 0)
            scores = jnp.where(row < length, scores + added, -1e30)
            top = jnp.max(scores, axis=0, keepdims=True)
            probs = jnp.exp(scores - top)
            probs = probs * (1.0 / jnp.sum(probs, axis=0, keepdims=True))
            product = probs * dot_nt(values, grads)
            delta = jnp.sum(product, axis=0, keepdims=True)
            grad_scores = product - probs * delta
            bias_out[head, first_row : first_row + seq_len, :] += grad_scores[:, :128]
            bias_out[head, first_row - 128 : first_row - 128 + seq_len, :] += grad_scores[:, 128:]
            scores_low = grad_scores.astype(bf16)
            key_part = dot_nn(scores_low, queries)
            value_part = dot_nn(probs.astype(bf16), grads)
            if block == 0:
                key_sum[...] = key_part
                value_sum[...] = value_part
            else:
                key_sum[...] += key_part
                value_sum[...] += value_part
            query_grad = dot_tn(keys, scores_low) * head_size ** (-0.5)
            joined[span, lanes] = query_grad.T.astype(bf16)
        joined[:, width_heads + head * head_size : width_heads + (head + 1) * head_size] = key_sum[
            ...
        ].astype(bf16)
        joined[
            :, 2 * width_heads + head * head_size : 2 * width_heads + (head + 1) * head_size
        ] = value_sum[...].astype(bf16)
    gain_out[...] = jnp.zeros_like(gain_out)
    for block in range(0, seq_len, 256):
        span = slice(block, block + 256)
        low = joined[span, :]
        wide = tokens[span, :].astype(f32)
        factor = lax.rsqrt(jnp.mean(wide * wide, axis=-1, keepdims=True) + epsilon)
        upstream = dot_nt(low, weight[...])
        spread = wide * factor
        gain_out[0:1, :] += jnp.sum(upstream * spread, axis=0, keepdims=True)
        middle = jnp.mean(upstream * wide, axis=-1, keepdims=True) * (factor * factor)
        back = factor * upstream - spread * middle + grad_in[span, :].astype(f32)
        grad_out[span, :] = back.astype(bf16)
        parts_out[span, :] = (low.astype(f32) * factor).astype(bf16)


def attend_back(meta, tokens, qkv, grad_heads, weight, bias, grad_in, heads, head_size):
    seq_len, width = tokens.shape
    return pl.pallas_call(
        functools.partial(attend_back_kernel, heads, head_size),
        out_shape=(
            jax.ShapeDtypeStruct((seq_len, width), bf16),
            jax.ShapeDtypeStruct((seq_len, 3 * heads * head_size), bf16),
            jax.ShapeDtypeStruct(bias.shape, f32),
            jax.ShapeDtypeStruct((8, width), f32),
        ),
        grid_spec=pltpu.PrefetchScalarGridSpec(
            num_scalar_prefetch=1,
            grid=(),
            in_specs=[whole_ref] * 6,
            out_specs=[whole_ref] * 4,
            scratch_shapes=[
                pltpu.VMEM((seq_len, head_size), f32),
                pltpu.VMEM((seq_len, head_size), f32),
                pltpu.VMEM((seq_len, 3 * heads * head_size), bf16),
            ],
        ),
        compiler_params=pltpu.CompilerParams(vmem_limit_bytes=vmem_limit),
        cost_estimate=pl.CostEstimate(
            flops=30 * 10**9, bytes_accessed=12 * 10**6, transcendentals=heads * seq_len * seq_len
        ),
        name="attend_back",
    )(meta, tokens, qkv, grad_heads, weight, bias, grad_in)


def body(
    tokens,
    lengths,
    expert_ids,
    buckets,
    norm1_gain,
    w_query,
    w_key,
    w_value,
    w_out,
    rel_bias,
    norm2_gain,
    w_router,
    w_gate,
    w_up,
    w_down,
    cotangent,
):
    seqs, span, width = tokens.shape
    count = lax.axis_size("shard")
    reps = lax.axis_size("rep")
    me = lax.axis_index("shard")
    rep = lax.axis_index("rep")
    seq_len = span * count
    expert_count, unit_count, _ = w_gate.shape
    heads = rel_bias.shape[1]
    head_size = w_query.shape[1] // (count * heads)
    each = heads * head_size
    feats = w_query.shape[0]
    cut = feats // reps
    row_count = seqs * span
    capacity = 10 * row_count // (4 * expert_count)
    place = ring_place(me, count)
    distances = jnp.arange(count, dtype=jnp.int32)
    owners = ring_index((place + distances) % count, count)
    distance_of = (ring_place(distances, count) - place) % count
    metas = [
        jnp.concatenate([lengths[s : s + 1], owners, me[None]]).astype(jnp.int32)
        for s in range(seqs)
    ]

    token_pieces = [ring_gather(tokens[0], count)]
    gain_one = norm1_gain.astype(f32)
    own_qkv = jnp.stack([w_query, w_key, w_value], axis=1)
    own_cut = lax.dynamic_slice_in_dim(own_qkv, rep * cut, cut, 0).astype(f32)
    own_cut = own_cut * lax.dynamic_slice_in_dim(gain_one, rep * cut, cut, 0)[:, None, None]
    own_cut = own_cut.astype(bf16).reshape(cut, 3, count, each).transpose(2, 0, 1, 3)
    qkv_weight = lax.all_to_all(
        own_cut.reshape(count, cut, 3 * each), "shard", split_axis=0, concat_axis=0, tiled=True
    )
    qkv_weight = rep_gather(qkv_weight, reps, rep).transpose(1, 0, 2, 3).reshape(width, 3 * each)

    positions = me * span + jnp.arange(span, dtype=jnp.int32)
    live_mask = positions[None, :] < lengths[:, None]
    pair_ids = expert_ids.reshape(row_count, 2)
    kept = assign_slots(
        pair_ids.reshape(-1),
        jnp.repeat(live_mask.reshape(row_count).astype(jnp.int32), 2),
        expert_count,
        capacity,
    ).reshape(row_count, 2)
    choose = pair_ids[:, :, None] == jnp.arange(expert_count, dtype=jnp.int32)[None, None, :]
    code = jnp.sum(choose.astype(f32) * (1.0 + kept.astype(f32))[:, :, None], axis=1)

    def line(values):
        flat = values.reshape(-1).astype(bf16)
        return jnp.pad(flat, (0, width - flat.shape[0]))[None]

    extras = jnp.concatenate(
        [
            line(code),
            line(jnp.concatenate([norm2_gain, w_router.reshape(-1)])),
            jnp.zeros((14, width), bf16),
        ],
        axis=0,
    )
    out_cut = lax.dynamic_slice_in_dim(w_out, rep * cut, cut, 0)
    packed = jnp.concatenate([tokens[1], out_cut, extras], axis=0)
    packed_pieces = ring_gather(packed, count)
    packed_list = pieces_in_order(packed_pieces, count)
    token_pieces.append([(d, 0, piece) for d, piece in enumerate(packed_list)])
    out_parts = jnp.stack([piece[span : span + cut] for piece in packed_list])
    out_weight = rep_gather(out_parts, reps, rep).transpose(1, 0, 2, 3).reshape(width, width)
    small = jnp.stack([piece[span + cut : span + cut + 2] for piece in packed_list])
    small = jnp.take(small, distance_of, axis=0)
    codes = small[:, 0, : row_count * expert_count].astype(f32)
    codes = codes.reshape(count, seqs, span, expert_count).transpose(1, 0, 2, 3)
    codes = codes.reshape(seqs, seq_len, expert_count)
    codes = jnp.pad(codes, ((0, 0), (0, 0), (0, 128 - expert_count)))
    gain_two = small[:, 1, :feats].astype(f32).reshape(1, width)
    router_weight = small[:, 1, feats : feats * (1 + expert_count)].reshape(width, expert_count)
    router_weight = jnp.pad(router_weight, ((0, 0), (0, 128 - expert_count)))

    bucket_count = rel_bias.shape[0]
    bucket_hot = (
        buckets[:, None] == jnp.arange(bucket_count, dtype=jnp.int32)[None, :]
    ).astype(f32)
    bias_vec = jnp.einsum("rb,bh->hr", bucket_hot, rel_bias.astype(f32), precision=highest)
    bias_width = 2 * seq_len - 128
    bias = toeplitz_rows(bias_vec, 128, bias_width)
    bias_turned = jnp.swapaxes(bias, 1, 2)

    cot_all = []
    for s in range(seqs):
        pieces = pieces_in_order(ring_gather(cotangent[s], count), count)
        joined = jnp.take(jnp.stack(pieces), distance_of, axis=0)
        cot_all.append(joined.reshape(seq_len, width))
    expert_weights = [
        weight.reshape(expert_count * unit_count, width) for weight in (w_gate, w_up, w_down)
    ]
    token_all, qkv_all, context_all = [], [], []
    for s in range(seqs):
        token_rows, qkv, context = attend(
            metas[s], token_pieces[s], qkv_weight, bias, span, heads, head_size
        )
        token_all.append(token_rows)
        qkv_all.append(qkv)
        context_all.append(pieces_in_order(ring_gather(context, count), count))
    results = []
    for s in range(seqs):
        results.append(
            experts(
                metas[s],
                token_all[s],
                context_all[s],
                out_weight,
                gain_two,
                router_weight,
                codes[s],
                cot_all[s],
                expert_weights,
                span,
                expert_count,
            )
        )
    grad_head_all = []
    for s in range(seqs):
        heads_part = results[s][7]
        right, left = ring_sum(lambda d: heads_part[d], count)
        total = heads_part[0].astype(f32) + right.astype(f32) + left.astype(f32)
        grad_head_all.append(total.astype(bf16))
    mix_parts = [result[5] for result in results]

    def rows_of(parts, distance):
        start = owners[distance] * span
        return [lax.dynamic_slice_in_dim(part, start, span, 0) for part in parts]

    right, left = ring_sum(lambda d: jnp.concatenate(rows_of(mix_parts, d), axis=0), count)
    mix_own = jnp.concatenate(rows_of(mix_parts, 0), axis=0).astype(f32)
    mix_own = mix_own + right.astype(f32) + left.astype(f32)
    block_out = (live_mask.reshape(row_count, 1).astype(f32) * mix_own).astype(bf16)
    block_out = block_out.reshape(seqs, span, width)

    def weight_grad(spots, sides):
        total = sum(
            jnp.einsum("clf,ld->cfd", results[s][spots], sides[s], preferred_element_type=f32)
            for s in range(seqs)
        )
        total = total.astype(bf16).reshape(expert_count * unit_count, width)
        return rep_total(total, reps, rep).reshape(expert_count, unit_count, width)

    normed_all = [result[1] for result in results]
    total_down = weight_grad(2, cot_all)
    total_gate = weight_grad(3, normed_all)
    total_up = weight_grad(4, normed_all)

    out_grad = sum(
        jnp.einsum("lc,ld->cd", results[s][0], results[s][6], preferred_element_type=f32)
        for s in range(seqs)
    ).astype(bf16)
    out_grad = out_grad.reshape(count, reps, cut, width)
    out_grad = rep_scatter(out_grad.transpose(1, 0, 2, 3), reps, rep)
    right, left = ring_sum(lambda d: out_grad[d], count)
    out_grad = add_low(out_grad[0].astype(f32) + right.astype(f32), left)
    total_out = rep_gather(out_grad, reps, rep).reshape(feats, width).astype(f32)

    backs = [
        attend_back(
            metas[s],
            token_all[s],
            qkv_all[s],
            grad_head_all[s],
            qkv_weight,
            bias_turned,
            results[s][6],
            heads,
            head_size,
        )
        for s in range(seqs)
    ]
    grad_tokens = []
    for s in range(seqs):
        grads = backs[s][0]
        right, left = ring_sum(lambda d: rows_of([grads], d)[0], count)
        own = rows_of([grads], 0)[0].astype(f32)
        grad_tokens.append(own + right.astype(f32) + left.astype(f32))
    grad_tokens = jnp.stack(grad_tokens)

    qkv_grad = sum(
        jnp.einsum("ld,lc->dc", token_all[s], backs[s][1], preferred_element_type=f32)
        for s in range(seqs)
    ).astype(bf16)
    qkv_grad = qkv_grad.reshape(count, reps, cut, 3 * each).transpose(1, 0, 2, 3)
    qkv_grad = rep_scatter(qkv_grad, reps, rep)
    qkv_grad = lax.all_to_all(qkv_grad, "shard", split_axis=0, concat_axis=0, tiled=True)
    qkv_grad = rep_gather(qkv_grad, reps, rep)
    qkv_grad = qkv_grad.reshape(reps, count, cut, 3, each).transpose(3, 0, 2, 1, 4)
    qkv_grad = qkv_grad.reshape(3, feats, width).astype(f32) * gain_one[None, :, None]

    router_grad = sum(
        jnp.einsum("ld,le->de", normed_all[s], results[s][8], preferred_element_type=f32)
        for s in range(seqs)
    )[:, :expert_count]
    gain_two_grad = sum(result[9][0] for result in results)
    gain_one_grad = sum(back[3][0] for back in backs)
    table = jnp.swapaxes(sum(back[2] for back in backs), 1, 2)
    offset_sums = diagonal_sums(table, 128, bias_width)
    bias_grad = jnp.einsum("hr,rb->bh", offset_sums, bucket_hot, precision=highest)
    bias_size = bucket_count * heads
    flat = jnp.concatenate(
        [
            gain_one_grad.reshape(count, feats),
            gain_two_grad.reshape(count, feats),
            router_grad.reshape(count, feats * expert_count),
        ],
        axis=1,
    ).reshape(-1)
    flat = jnp.concatenate([flat, bias_grad.reshape(-1)])
    for bit in bits_of(reps):
        flat = flat + swap(flat, "rep", reps, bit)
    total_bias = flat[-bias_size:].reshape(bucket_count, heads)
    flat = flat[:-bias_size]
    for bit in bits_of(count):
        flat = flat + swap(flat, "shard", count, bit)
    flat = lax.dynamic_index_in_dim(flat.reshape(count, -1), me, 0, keepdims=False)
    total_gain_one = flat[:feats] / gain_one
    total_gain_two = flat[feats : 2 * feats]
    total_router = flat[2 * feats :].reshape(feats, expert_count)
    return (
        block_out,
        grad_tokens,
        total_gain_one,
        qkv_grad[0],
        qkv_grad[1],
        qkv_grad[2],
        total_out,
        total_bias,
        total_gain_two,
        total_router,
        total_gate,
        total_up,
        total_down,
    )


def solution(mesh):
    rows = P("rep", "shard", None)
    first = P("shard")
    weight = P("shard", None)
    expert = P(None, "shard", None)
    return jax.shard_map(
        body,
        mesh=mesh,
        in_specs=(rows, P("rep"), rows, P(), first, weight, weight, weight, weight)
        + (P(None, "shard"), first, weight, expert, expert, expert, rows),
        out_specs=(rows, rows, first, weight, weight, weight, weight)
        + (P(None, "shard"), first, weight, expert, expert, expert),
        check_vma=False,
    )
```

time: 3940 us -> 738 us (0.19)
  waiting for transfers between devices: 3110 us -> 166 us
  matrix products: 274 us -> 34.4 us
  local copies, waits for them, and re-layouts: 373 us -> 134 us
  starting transfers between devices: 0.8 us -> 153 us
  Pallas kernels: 0 us -> 145 us
  blocking collectives: 89.1 us -> 0 us
    reduce_scatter x9 -> x0, waiting for transfers between devices: 1540 us -> none  [the longest x1 378 us: body(): lax.psum_scatter(full_gate.astype(jnp.bfloat16), 'shard', scatter_dimensi...]
    all_gather x9 -> x0, waiting for transfers between devices: 1370 us -> none  [the longest x1 429 us: body(): up_piece = lax.all_gather(w_up, 'shard', axis=1, tiled=True)]
    dot_general x45 -> x14, matrix products: 274 us -> 34.4 us  [the longest x6 20.1 us: weight_grad(): jnp.einsum('clf,ld->cfd', results[s][spots], sides[s], preferred_element_...]
    ppermute x0 -> x122, waiting for transfers between devices: none -> 166 us  [the longest x96 83.2 us: ring_send(): return lax.ppermute(value, 'shard', pairs)]
    pallas_call x0 -> x6, Pallas kernels: none -> 145 us  [the longest x2 87.7 us: experts(): pl.pallas_call(functools.partial(experts_kernel, count, span, expert_coun...]
    ppermute x0 -> x122, starting transfers between devices: none -> 142 us  [the longest x96 81.1 us: ring_send(): return lax.ppermute(value, 'shard', pairs)]
    psum x1 -> x0, waiting for transfers between devices: 139 us -> none  [body(): lax.psum(share_query.astype(jnp.bfloat16), 'rep').astype(jnp.float32)]
    slice x16 -> x1, local copies, waits for them, and re-layouts: 81.3 us -> 1.67 us  [toeplitz_rows(): return shaped[..., :col_count]]
  transfers between devices with their start and end apart: 20 -> 124, of which waited for: 18 -> 38; matrix products, arithmetic and copies ran while one was open for 8% -> 33% of each run, Pallas kernels for 0% -> 14%
where the time goes in v1:
time: 738 us; the launch traced here: 724 us
  waiting for transfers between devices  166 us (22%)
  starting transfers between devices  153 us (21%)
  Pallas kernels  145 us (20%)
  local copies, waits for them, and re-layouts  134 us (18%)
  other arithmetic  84.1 us (11%)
  matrix products  34.4 us (5%)
  between operations  7.8 us (1%)
    pallas_call x2, Pallas kernels, experts(): pl.pallas_call(functools.partial(experts_kernel, count, span, expert_coun...  87.7 us
    ppermute x96, waiting for transfers between devices, ring_send(): return lax.ppermute(value, 'shard', pairs)  83.2 us
    ppermute x26, waiting for transfers between devices, swap(): return lax.ppermute(value, axis, [(i, i ^ bit) for i in range(count)])  83 us
    ppermute x96, starting transfers between devices, ring_send(): return lax.ppermute(value, 'shard', pairs)  81.1 us
    ppermute x26, starting transfers between devices, swap(): return lax.ppermute(value, axis, [(i, i ^ bit) for i in range(count)])  61 us
    unnamed x204, local copies, waits for them, and re-layouts  58.5 us
    pallas_call x2, Pallas kernels, attend_back(): pl.pallas_call(functools.partial(attend_back_kernel, heads, head_size), o...  37.6 us
    convert_element_type x29, other arithmetic, add_low(): return (left.astype(f32) + right.astype(f32)).astype(bf16)  31.2 us
  transfers between devices with their start and end apart: 124, of which 38 were waited for; matrix products, arithmetic and copies ran while one was open for 33% of the time, Pallas kernels for 14%

profile of v1, /device:TPU:1, one launch (start us, length us, event | category | flops | bytes accessed | tf_op | source)
XLA Modules:
  0.0 724.4 jit_solution(7344844501885411243)
XLA Ops:
  15.6 4.6 all-to-all-start
  56.7 3.7 collective-permute-done.1.refs_2_
  67.6 4.5 collective-permute-done.2.refs_3_
  74.2 4.5 collective-permute-done.29
  84.2 7.8 %collective-permute-start.9 = (bf16[2,8,32,384]{3,2,1,0:T(8,128)(2,1)}, bf16[2,8,32,384]{3,2,1,0:T(8,128)(2,1)}, u32[]{:S(2)}, u32[]{:S(2)}) collective-permute-start(bf16[2,8,32,384]{3,2,1,0:T(8,128)(2,1)} %maximum_bitcast_fusion.1), channel_id=1, source_target_pairs={{0,1},{1,0},{2,3},{3,2},{4,5},{5,4},{6,7},{7,6},{8,9},{9,8},{10,11... | collective-permute-start | bytes 1179656 | tf_op jit(solution)/shard_map/ppermute | solution.py:91
  100.3 5.5 collective-permute-done.34
  121.7 3.6 gather_fusion.2
  125.3 4.1 broadcast_select_fusion.1
  131.7 9.8 %attend.2 = (bf16[1024,1024]{1,0:T(8,128)(2,1)}, bf16[6,1024,64]{2,1,0:T(8,128)(2,1)}, bf16[1024,128]{1,0:T(8,128)(2,1)}) custom-call(s32[10]{0:T(128)} %get-tuple-element.260.meta, bf16[128,1024]{1,0:T(8,128)(2,1)} %get-tuple-element.240.refs_0_, bf16[128,1024]{1,0:T(8,128)(2,1)} %copy-done.67, bf16[128,1024]{1,0:T(8,128)(2,1)} %copy-done.69, ...), custom_call_target="tpu_custom_call" | custom-call | flops 20000000000 | bytes 8000000 | tf_op jit(solution)/shard_map/attend/pallas_call | solution.py:219
  151.0 9.9 %attend.3 = (bf16[1024,1024]{1,0:T(8,128)(2,1)}, bf16[6,1024,64]{2,1,0:T(8,128)(2,1)}, bf16[1024,128]{1,0:T(8,128)(2,1)}) custom-call(s32[10]{0:T(128)} %get-tuple-element.261.meta, bf16[176,1024]{1,0:T(8,128)(2,1)} %copy-done.42, bf16[176,1024]{1,0:T(8,128)(2,1)} %collective-permute-done.18.refs_1_, bf16[176,1024]{1,0:T(8,128)(2,1)} %collective-permute-done.19.refs_2_, ...), custom_call_target="tpu_custom_call" | custom-call | flops 20000000000 | bytes 8000000 | tf_op jit(solution)/shard_map/attend/pallas_call | solution.py:219
  174.1 11.5 %collective-permute-start.26 = (bf16[2,8,32,1024]{3,2,1,0:T(8,128)(2,1)}, bf16[2,8,32,1024]{3,2,1,0:T(8,128)(2,1)S(1)}, u32[]{:S(2)}, u32[]{:S(2)}) collective-permute-start(bf16[2,8,32,1024]{3,2,1,0:T(8,128)(2,1)} %maximum_bitcast_fusion), channel_id=1, source_target_pairs={{0,1},{1,0},{2,3},{3,2},{4,5},{5,4},{6,7},{7,6},{8,9},{9,8},{10,11... | collective-permute-start | bytes 3145736 | tf_op jit(solution)/shard_map/ppermute | solution.py:91
  191.8 4.2 collective-permute-done.12.refs_3_
  210.3 43.9 %experts.3 = (bf16[1024,1024]{1,0:T(8,128)(2,1)}, bf16[1024,1024]{1,0:T(8,128)(2,1)}, bf16[2,1024,704]{2,1,0:T(8,128)(2,1)}, bf16[2,1024,704]{2,1,0:T(8,128)(2,1...) custom-call(s32[10]{0:T(128)} %get-tuple-element.261.meta, ...), custom_call_target="tpu_custom_call" | custom-call | flops 22011707392 | bytes 40000000 | tf_op jit(solution)/shard_map/experts/pallas_call | solution.py:370
  258.2 43.9 %experts.2 = (bf16[1024,1024]{1,0:T(8,128)(2,1)}, bf16[1024,1024]{1,0:T(8,128)(2,1)}, bf16[2,1024,704]{2,1,0:T(8,128)(2,1)}, bf16[2,1024,704]{2,1,0:T(8,128)(2,1...) custom-call(s32[10]{0:T(128)} %get-tuple-element.260.meta, ...), custom_call_target="tpu_custom_call" | custom-call | flops 22011707392 | bytes 40000000 | tf_op jit(solution)/shard_map/experts/pallas_call | solution.py:370
  314.3 4.8 fusion.69
  327.3 3.6 add_convert_fusion.2
  369.5 6.5 collective-permute-start.101
  375.9 7.1 collective-permute-done.82
  384.0 6.5 collective-permute-start.113
  401.3 18.7 %attend_back.3 = (bf16[1024,1024]{1,0:T(8,128)(2,1)}, bf16[1024,384]{1,0:T(8,128)(2,1)}, f32[2,1920,128]{2,1,0:T(8,128)}, f32[8,1024]{1,0:T(8,128)}) custom-call(s32[10]{0:T(128)} %get-tuple-element.261.meta, bf16[1024,1024]{1,0:T(8,128)(2,1)} %get-tuple-element.51.tokens, bf16[6,1024,64]{2,1,0:T(8,128)(2,1)} %get-tuple-element.58.qkv, ...), custom_call_target="tpu_custom_call" | custom-call | flops 30000001024 | bytes 12000000 | tf_op jit(solution)/shard_map/attend_back/pallas_call | solution.py:504
  420.9 18.9 %attend_back.2 = (bf16[1024,1024]{1,0:T(8,128)(2,1)}, bf16[1024,384]{1,0:T(8,128)(2,1)}, f32[2,1920,128]{2,1,0:T(8,128)}, f32[8,1024]{1,0:T(8,128)}) custom-call(s32[10]{0:T(128)} %get-tuple-element.260.meta, bf16[1024,1024]{1,0:T(8,128)(2,1)} %get-tuple-element.48.tokens, bf16[6,1024,64]{2,1,0:T(8,128)(2,1)} %get-tuple-element.54.qkv, ...), custom_call_target="tpu_custom_call" | custom-call | flops 30000001024 | bytes 12000000 | tf_op jit(solution)/shard_map/attend_back/pallas_call | solution.py:504
  447.2 4.2 reshape.529
  451.3 20.9 %dynamic-update-slice.3 = f32[2,262144]{1,0:T(2,128)} dynamic-update-slice(f32[2,262144]{1,0:T(2,128)} %dynamic-update-slice.2, f32[2,262016]{1,0:T(2,128)} %reshape.529, s32[]{} %constant.297, s32[]{} %constant.299) | dynamic-update-slice | bytes 4192260
  478.8 6.3 collective-permute-start.92
  515.5 3.8 collective-permute-start.116
  523.2 9.6 %collective-permute-done.58 = bf16[256,1024]{1,0:T(8,128)(2,1)S(1)} collective-permute-done((bf16[256,1024]{1,0:T(8,128)(2,1)S(1)}, bf16[256,1024]{1,0:T(8,128)(2,1)S(1)}, u32[]{:S(2)}, u32[]{:S(2)}) %collective-permute-start.58) | collective-permute-done | bytes 524320 | tf_op jit(solution)/shard_map/ppermute | solution.py:41
  543.1 4.1 collective-permute-done.69
  569.1 6.1 all-to-all-start.1
  590.2 5.7 collective-permute-done.106
  607.1 71.3 %collective-permute-done.111 = bf16[1,32,1024]{2,1,0:T(8,128)(2,1)S(1)} collective-permute-done((bf16[1,32,1024]{2,1,0:T(8,128)(2,1)S(1)}, bf16[1,32,1024]{2,1,0:T(8,128)(2,1)S(1)}, u32[]{:S(2)}, u32[]{:S(2)}) %collective-permute-start.111) | collective-permute-done | bytes 65568 | tf_op jit(solution)/shard_map/ppermute | solution.py:91
  679.0 4.6 collective-permute-start.112
  686.0 5.5 collective-permute-done.99
  (661 shorter events, 347.1 us)
Async XLA Ops:
  2.9 38.0 %collective-permute-start.27 = (bf16[128,1024]{1,0:T(8,128)(2,1)}, bf16[128,1024]{1,0:T(8,128)(2,1)}, u32[]{:S(2)}, u32[]{:S(2)}) collective-permute-start(bf16[128,1024]{1,0:T(8,128)(2,1)} %get-tuple-element.236), channel_id=1, source_target_pairs={{0,4},{8,0},{16,8},{24,16},{28,24},{20,28},{12,20},{4,12},{1,5},{9... | collective-permute-start | bytes 786440 | tf_op jit(solution)/shard_map/ppermute | solution.py:41
  5.0 43.8 %collective-permute-start.30 = (bf16[128,1024]{1,0:T(8,128)(2,1)}, bf16[128,1024]{1,0:T(8,128)(2,1)}, u32[]{:S(2)}, u32[]{:S(2)}) collective-permute-start(bf16[128,1024]{1,0:T(8,128)(2,1)} %get-tuple-element.236), channel_id=1, source_target_pairs={{0,8},{8,16},{16,24},{24,28},{28,20},{20,12},{12,4},{4,0},{1,9},{9... | collective-permute-start | bytes 786440 | tf_op jit(solution)/shard_map/ppermute | solution.py:41
  5.0 39.0 %collective-permute-start.44 = (bf16[128,1024]{1,0:T(8,128)(2,1)}, bf16[128,1024]{1,0:T(8,128)(2,1)}, u32[]{:S(2)}, u32[]{:S(2)}) collective-permute-start(bf16[128,1024]{1,0:T(8,128)(2,1)} %get-tuple-element.239), channel_id=1, source_target_pairs={{0,4},{8,0},{16,8},{24,16},{28,24},{20,28},{12,20},{4,12},{1,5},{9... | collective-permute-start | bytes 786440 | tf_op jit(solution)/shard_map/ppermute | solution.py:41
  6.4 42.4 %collective-permute-start.47 = (bf16[128,1024]{1,0:T(8,128)(2,1)}, bf16[128,1024]{1,0:T(8,128)(2,1)S(1)}, u32[]{:S(2)}, u32[]{:S(2)}) collective-permute-start(bf16[128,1024]{1,0:T(8,128)(2,1)} %get-tuple-element.239), channel_id=1, source_target_pairs={{0,8},{8,16},{16,24},{24,28},{28,20},{20,12},{12,4},{4,0},{1,9},{9... | collective-permute-start | bytes 786440 | tf_op jit(solution)/shard_map/ppermute | solution.py:41
  12.9 32.8 %collective-permute-start.18 = (bf16[176,1024]{1,0:T(8,128)(2,1)S(1)}, bf16[176,1024]{1,0:T(8,128)(2,1)}, u32[]{:S(2)}, u32[]{:S(2)}) collective-permute-start(bf16[176,1024]{1,0:T(8,128)(2,1)S(1)} %concatenate.115.refs_0_), channel_id=1, source_target_pairs={{0,4},{8,0},{16,8},{24,16},{28,24},{20,28},{12,20},{4,12},{1,5},{9... | collective-permute-start | bytes 1081352 | tf_op jit(solution)/shard_map/ppermute | solution.py:41
  15.6 38.0 %all-to-all-start = ((bf16[8,32,384]{2,1,0:T(8,128)(2,1)}), bf16[8,32,384]{2,1,0:T(8,128)(2,1)S(1)}, u32[]{:S(2)}, u32[]{:S(2)}) async-start(bf16[8,32,384]{2,1,0:T(8,128)(2,1)} %reshape.510), calls=%async_computation | async-start | bytes 393216 | tf_op jit(solution)/shard_map/all_to_all | solution.py:578
  84.2 45.2 %collective-permute-start.9 = (bf16[2,8,32,384]{3,2,1,0:T(8,128)(2,1)}, bf16[2,8,32,384]{3,2,1,0:T(8,128)(2,1)}, u32[]{:S(2)}, u32[]{:S(2)}) collective-permute-start(bf16[2,8,32,384]{3,2,1,0:T(8,128)(2,1)} %maximum_bitcast_fusion.1), channel_id=1, source_target_pairs={{0,1},{1,0},{2,3},{3,2},{4,5},{5,4},{6,7},{7,6},{8,9},{9,8},{10,11... | collective-permute-start | bytes 1179656 | tf_op jit(solution)/shard_map/ppermute | solution.py:91
  92.7 50.2 %collective-permute-start.20 = (bf16[176,1024]{1,0:T(8,128)(2,1)}, bf16[176,1024]{1,0:T(8,128)(2,1)}, u32[]{:S(2)}, u32[]{:S(2)}) collective-permute-start(bf16[176,1024]{1,0:T(8,128)(2,1)} %collective-permute-done.19.refs_2_), channel_id=1, source_target_pairs={{0,4},{8,0},{16,8},{24,16},{28,24},{20,28},{12,20},{4,12},{1,5},{9... | collective-permute-start | bytes 1081352 | tf_op jit(solution)/shard_map/ppermute | solution.py:41
  93.0 51.9 %collective-permute-start.24 = (bf16[176,1024]{1,0:T(8,128)(2,1)}, bf16[176,1024]{1,0:T(8,128)(2,1)}, u32[]{:S(2)}, u32[]{:S(2)}) collective-permute-start(bf16[176,1024]{1,0:T(8,128)(2,1)} %collective-permute-done.23.refs_6_), channel_id=1, source_target_pairs={{0,8},{8,16},{16,24},{24,28},{28,20},{20,12},{12,4},{4,0},{1,9},{9... | collective-permute-start | bytes 1081352 | tf_op jit(solution)/shard_map/ppermute | solution.py:41
  148.0 39.8 %collective-permute-start.11 = (bf16[1024,128]{1,0:T(8,128)(2,1)S(1)}, bf16[1024,128]{1,0:T(8,128)(2,1)}, u32[]{:S(2)}, u32[]{:S(2)}) collective-permute-start(bf16[1024,128]{1,0:T(8,128)(2,1)S(1)} %collective-permute-done.10.refs_1_), channel_id=1, source_target_pairs={{0,4},{8,0},{16,8},{24,16},{28,24},{20,28},{12,20},{4,12},{1,5},{9... | collective-permute-start | bytes 786440 | tf_op jit(solution)/shard_map/ppermute | solution.py:41
  149.0 40.0 %collective-permute-start.14 = (bf16[1024,128]{1,0:T(8,128)(2,1)}, bf16[1024,128]{1,0:T(8,128)(2,1)}, u32[]{:S(2)}, u32[]{:S(2)}) collective-permute-start(bf16[1024,128]{1,0:T(8,128)(2,1)} %collective-permute-done.13.refs_7_), channel_id=1, source_target_pairs={{0,8},{8,16},{16,24},{24,28},{28,20},{20,12},{12,4},{4,0},{1,9},{9... | collective-permute-start | bytes 786440 | tf_op jit(solution)/shard_map/ppermute | solution.py:41
  174.1 34.0 %collective-permute-start.26 = (bf16[2,8,32,1024]{3,2,1,0:T(8,128)(2,1)}, bf16[2,8,32,1024]{3,2,1,0:T(8,128)(2,1)S(1)}, u32[]{:S(2)}, u32[]{:S(2)}) collective-permute-start(bf16[2,8,32,1024]{3,2,1,0:T(8,128)(2,1)} %maximum_bitcast_fusion), channel_id=1, source_target_pairs={{0,1},{1,0},{2,3},{3,2},{4,5},{5,4},{6,7},{7,6},{8,9},{9,8},{10,11... | collective-permute-start | bytes 3145736 | tf_op jit(solution)/shard_map/ppermute | solution.py:91
  256.8 99.5 %collective-permute-start.56 = (bf16[128,1024]{1,0:T(8,128)(2,1)}, bf16[128,1024]{1,0:T(8,128)(2,1)}, u32[]{:S(2)}, u32[]{:S(2)}) collective-permute-start(bf16[128,1024]{1,0:T(8,128)(2,1)} %get-tuple-element.209), channel_id=1, source_target_pairs={{0,4},{8,0},{16,8},{24,16},{28,24},{20,28},{12,20},{4,12},{1,5},{9... | collective-permute-start | bytes 786440 | tf_op jit(solution)/shard_map/ppermute | solution.py:41
  304.9 53.6 %collective-permute-start.52 = (bf16[128,1024]{1,0:T(8,128)(2,1)}, bf16[128,1024]{1,0:T(8,128)(2,1)}, u32[]{:S(2)}, u32[]{:S(2)}) collective-permute-start(bf16[128,1024]{1,0:T(8,128)(2,1)} %get-tuple-element.205), channel_id=1, source_target_pairs={{0,8},{8,16},{16,24},{24,28},{28,20},{20,12},{12,4},{4,0},{1,9},{9... | collective-permute-start | bytes 786440 | tf_op jit(solution)/shard_map/ppermute | solution.py:41
  307.1 43.0 %collective-permute-start.76 = (bf16[512,128]{1,0:T(8,128)(2,1)}, bf16[512,128]{1,0:T(8,128)(2,1)}, u32[]{:S(2)}, u32[]{:S(2)}) collective-permute-start(bf16[512,128]{1,0:T(8,128)(2,1)} %get-tuple-element.195), channel_id=1, source_target_pairs={{0,8},{8,16},{16,24},{24,28},{28,20},{20,12},{12,4},{4,0},{1,9},{9... | collective-permute-start | bytes 393224 | tf_op jit(solution)/shard_map/ppermute | solution.py:41
  307.4 44.0 %collective-permute-start.80 = (bf16[512,128]{1,0:T(8,128)(2,1)}, bf16[512,128]{1,0:T(8,128)(2,1)}, u32[]{:S(2)}, u32[]{:S(2)}) collective-permute-start(bf16[512,128]{1,0:T(8,128)(2,1)} %get-tuple-element.196), channel_id=1, source_target_pairs={{0,4},{8,0},{16,8},{24,16},{28,24},{20,28},{12,20},{4,12},{1,5},{9... | collective-permute-start | bytes 393224 | tf_op jit(solution)/shard_map/ppermute | solution.py:41
  310.4 43.3 %collective-permute-start.60 = (bf16[512,128]{1,0:T(8,128)(2,1)}, bf16[512,128]{1,0:T(8,128)(2,1)}, u32[]{:S(2)}, u32[]{:S(2)}) collective-permute-start(bf16[512,128]{1,0:T(8,128)(2,1)} %get-tuple-element.175), channel_id=1, source_target_pairs={{0,8},{8,16},{16,24},{24,28},{28,20},{20,12},{12,4},{4,0},{1,9},{9... | collective-permute-start | bytes 393224 | tf_op jit(solution)/shard_map/ppermute | solution.py:41
  358.5 33.6 %collective-permute-start.57 = (bf16[256,1024]{1,0:T(8,128)(2,1)S(1)}, bf16[256,1024]{1,0:T(8,128)(2,1)S(1)}, u32[]{:S(2)}, u32[]{:S(2)}) collective-permute-start(bf16[256,1024]{1,0:T(8,128)(2,1)S(1)} %pad_maximum_fusion.7), channel_id=1, source_target_pairs={{0,4},{8,0},{16,8},{24,16},{28,24},{20,28},{12,20},{4,12},{1,5},{9... | collective-permute-start | bytes 1572872 | tf_op jit(solution)/shard_map/ppermute | solution.py:41
  369.5 143.5 %collective-permute-start.101 = (bf16[2,8,32,1024]{3,2,1,0:T(8,128)(2,1)}, bf16[2,8,32,1024]{3,2,1,0:T(8,128)(2,1)}, u32[]{:S(2)}, u32[]{:S(2)}) collective-permute-start(bf16[2,8,32,1024]{3,2,1,0:T(8,128)(2,1)} %bitcast.461), channel_id=1, source_target_pairs={{0,1},{1,0},{2,3},{3,2},{4,5},{5,4},{6,7},{7,6},{8,9},{9,8},{10,11... | collective-permute-start | bytes 3145736 | tf_op jit(solution)/shard_map/ppermute | solution.py:91
  384.0 167.3 %collective-permute-start.113 = (bf16[704,1024]{1,0:T(8,128)(2,1)}, bf16[704,1024]{1,0:T(8,128)(2,1)}, u32[]{:S(2)}, u32[]{:S(2)}) collective-permute-start(bf16[704,1024]{1,0:T(8,128)(2,1)} %dynamic-slice_bitcast_fusion.2), channel_id=1, source_target_pairs={{0,1},{1,0},{2,3},{3,2},{4,5},{5,4},{6,7},{7,6},{8,9},{9,8},{10,11... | collective-permute-start | bytes 4325384 | tf_op jit(solution)/shard_map/ppermute | solution.py:91
  393.9 26.1 %collective-permute-start.67 = (bf16[1024,128]{1,0:T(8,128)(2,1)}, bf16[1024,128]{1,0:T(8,128)(2,1)S(1)}, u32[]{:S(2)}, u32[]{:S(2)}) collective-permute-start(bf16[1024,128]{1,0:T(8,128)(2,1)} %get-tuple-element.170), channel_id=1, source_target_pairs={{0,4},{8,0},{16,8},{24,16},{28,24},{20,28},{12,20},{4,12},{1,5},{9... | collective-permute-start | bytes 786440 | tf_op jit(solution)/shard_map/ppermute | solution.py:41
  485.8 29.7 %collective-permute-start.84 = (bf16[64,1024]{1,0:T(8,128)(2,1)}, bf16[64,1024]{1,0:T(8,128)(2,1)}, u32[]{:S(2)}, u32[]{:S(2)}) collective-permute-start(bf16[64,1024]{1,0:T(8,128)(2,1)} %get-tuple-element.185), channel_id=1, source_target_pairs={{0,8},{8,16},{16,24},{24,28},{28,20},{20,12},{12,4},{4,0},{1,9},{9... | collective-permute-start | bytes 393224 | tf_op jit(solution)/shard_map/ppermute | solution.py:41
  486.6 32.7 %collective-permute-start.88 = (bf16[64,1024]{1,0:T(8,128)(2,1)}, bf16[64,1024]{1,0:T(8,128)(2,1)}, u32[]{:S(2)}, u32[]{:S(2)}) collective-permute-start(bf16[64,1024]{1,0:T(8,128)(2,1)} %get-tuple-element.188), channel_id=1, source_target_pairs={{0,4},{8,0},{16,8},{24,16},{28,24},{20,28},{12,20},{4,12},{1,5},{9... | collective-permute-start | bytes 393224 | tf_op jit(solution)/shard_map/ppermute | solution.py:41
  515.5 37.8 %collective-permute-start.116 = (bf16[704,1024]{1,0:T(8,128)(2,1)S(1)}, bf16[704,1024]{1,0:T(8,128)(2,1)S(1)}, u32[]{:S(2)}, u32[]{:S(2)}) collective-permute-start(bf16[704,1024]{1,0:T(8,128)(2,1)S(1)} %copy-done.20), channel_id=1, source_target_pairs={{0,1},{1,0},{2,3},{3,2},{4,5},{5,4},{6,7},{7,6},{8,9},{9,8},{10,11... | collective-permute-start | bytes 4325384 | tf_op jit(solution)/shard_map/ppermute | solution.py:91
  547.7 49.4 %collective-permute-start.59 = (bf16[256,1024]{1,0:T(8,128)(2,1)}, bf16[256,1024]{1,0:T(8,128)(2,1)}, u32[]{:S(2)}, u32[]{:S(2)}) collective-permute-start(bf16[256,1024]{1,0:T(8,128)(2,1)} %add_convert_fusion.9), channel_id=1, source_target_pairs={{0,4},{8,0},{16,8},{24,16},{28,24},{20,28},{12,20},{4,12},{1,5},{9... | collective-permute-start | bytes 1572872 | tf_op jit(solution)/shard_map/ppermute | solution.py:41
  551.3 26.4 %collective-permute-start.86 = (bf16[128,1024]{1,0:T(8,128)(2,1)}, bf16[128,1024]{1,0:T(8,128)(2,1)}, u32[]{:S(2)}, u32[]{:S(2)}) collective-permute-start(bf16[128,1024]{1,0:T(8,128)(2,1)} %get-tuple-element.181), channel_id=1, source_target_pairs={{0,8},{8,16},{16,24},{24,28},{28,20},{20,12},{12,4},{4,0},{1,9},{9... | collective-permute-start | bytes 786440 | tf_op jit(solution)/shard_map/ppermute | solution.py:41
  553.3 25.9 %collective-permute-start.90 = (bf16[128,1024]{1,0:T(8,128)(2,1)}, bf16[128,1024]{1,0:T(8,128)(2,1)}, u32[]{:S(2)}, u32[]{:S(2)}) collective-permute-start(bf16[128,1024]{1,0:T(8,128)(2,1)} %get-tuple-element.182), channel_id=1, source_target_pairs={{0,4},{8,0},{16,8},{24,16},{28,24},{20,28},{12,20},{4,12},{1,5},{9... | collective-permute-start | bytes 786440 | tf_op jit(solution)/shard_map/ppermute | solution.py:41
  569.1 115.6 %all-to-all-start.1 = ((bf16[8,32,384]{2,1,0:T(8,128)(2,1)}), bf16[8,32,384]{2,1,0:T(8,128)(2,1)}, u32[]{:S(2)}, u32[]{:S(2)}) async-start(bf16[8,32,384]{2,1,0:T(8,128)(2,1)} %fusion.34), calls=%async_computation.1 | async-start | bytes 393216 | tf_op jit(solution)/shard_map/all_to_all | solution.py:735
  585.8 108.4 %collective-permute-start.114 = (bf16[704,1024]{1,0:T(8,128)(2,1)S(1)}, bf16[704,1024]{1,0:T(8,128)(2,1)}, u32[]{:S(2)}, u32[]{:S(2)}) collective-permute-start(bf16[704,1024]{1,0:T(8,128)(2,1)S(1)} %fusion.2), channel_id=1, source_target_pairs={{0,2},{1,3},{2,0},{3,1},{4,6},{5,7},{6,4},{7,5},{8,10},{9,11},{10,... | collective-permute-start | bytes 4325384 | tf_op jit(solution)/shard_map/ppermute | solution.py:91
  601.8 103.1 %collective-permute-start.117 = (bf16[704,1024]{1,0:T(8,128)(2,1)S(1)}, bf16[704,1024]{1,0:T(8,128)(2,1)}, u32[]{:S(2)}, u32[]{:S(2)}) collective-permute-start(bf16[704,1024]{1,0:T(8,128)(2,1)S(1)} %fusion.1), channel_id=1, source_target_pairs={{0,2},{1,3},{2,0},{3,1},{4,6},{5,7},{6,4},{7,5},{8,10},{9,11},{10,... | collective-permute-start | bytes 4325384 | tf_op jit(solution)/shard_map/ppermute | solution.py:91
  603.0 104.7 %collective-permute-start.120 = (bf16[704,1024]{1,0:T(8,128)(2,1)}, bf16[704,1024]{1,0:T(8,128)(2,1)}, u32[]{:S(2)}, u32[]{:S(2)}) collective-permute-start(bf16[704,1024]{1,0:T(8,128)(2,1)} %fusion), channel_id=1, source_target_pairs={{0,2},{1,3},{2,0},{3,1},{4,6},{5,7},{6,4},{7,5},{8,10},{9,11},{10,... | collective-permute-start | bytes 4325384 | tf_op jit(solution)/shard_map/ppermute | solution.py:91
  604.4 74.0 %collective-permute-start.111 = (bf16[1,32,1024]{2,1,0:T(8,128)(2,1)S(1)}, bf16[1,32,1024]{2,1,0:T(8,128)(2,1)S(1)}, u32[]{:S(2)}, u32[]{:S(2)}) collective-permute-start(bf16[1,32,1024]{2,1,0:T(8,128)(2,1)S(1)} %fusion.43), channel_id=1, source_target_pairs={{0,2},{1,3},{2,0},{3,1},{4,6},{5,7},{6,4},{7,5},{8,10},{9,11},{10,... | collective-permute-start | bytes 196616 | tf_op jit(solution)/shard_map/ppermute | solution.py:91
  (176 other events, 1883.5 us)
